TPU v7x, 256 devices: a whole 4x4x8 slice. The times are simulated.
256 devices in a mesh: member: 32 (over y, z), space: 8 (over x, core).
Axes of the slice: x: 4, y: 4, z: 8, core: 2. Of those that a mesh axis runs over, the one named last changes fastest.
Arguments:
- starting_fields: bfloat16 [64, 80, 32, 360], P('member', None, 'space'), may hold values from -6 to 6
- conv_weight: bfloat16 [1, 9, 80, 80], replicated, may hold values from -0.21875 to 0.21875
- norm_gain: float32 [1, 80], replicated, may hold values from 0.1 to 1.9
- weight_in: bfloat16 [1, 320, 80], replicated, may hold values from -0.625 to 0.625
- weight_out: bfloat16 [1, 80, 320], replicated, may hold values from -0.3125 to 0.3125
- obs_count: int32 [8, 32], P('space', 'member'), may hold values from 1 to 256, 4096 in all within a row
- obs_point: int32 [8, 32, 256], P('space', 'member'), may hold values from 0 to 44
- obs_channel: int32 [8, 32, 256], P('space', 'member'), may hold values from 0 to 79
- obs_value: float32 [8, 32, 256], P('space', 'member'), may hold values from -6 to 6
- obs_precision: float32 [8, 32, 256], P('space', 'member'), may hold values from 0.1 to 1
Outputs:
- analysis: bfloat16 [64, 80, 32, 360], P('member', None, 'space')
Inputs may be any that keep to these rules, and one draw needn't show every extreme that they name: `obs_count`: in each band one tile has exactly 256 live slots, and the counts of a band sum to 4096.
All inputs are finite; a program needn't handle non-finite values. No bound on the sum of `obs_count` on one device may be relied on, other than what follows from the above.
Results may differ from a plain program's by a relative error of at most 0.0063.
Values may be sent and summed in bfloat16 or wider, within the bound.
No kernel may reach another device: no remote copies, remote signals or barrier semaphores. Data moves between devices by JAX's collectives and lax.ppermute only.
A program may use at most 128 MiB of HBM per device.

v0:
```python
import jax
import jax.numpy as jnp
from jax import lax
from jax.sharding import PartitionSpec as P

NS_STEPS = 6


HIGHEST_PRECISION = lax.Precision.HIGHEST
NEAR_WEIGHT = 0.5
EPSILON = 1e-06


def with_halo(block, sides, width):
    for axis, dim in sides:
        count = lax.axis_size(axis)
        forward = [(i, i + 1) for i in range(count - 1)]
        backward = [(target, source) for source, target in forward]
        low = lax.ppermute(
            lax.slice_in_dim(block, block.shape[dim] - width, None, axis=dim), axis, forward
        )
        high = lax.ppermute(lax.slice_in_dim(block, 0, width, axis=dim), axis, backward)
        block = jnp.concatenate([low, block, high], axis=dim)
    return block


def shifted_2(block, axis, distance):
    devices = range(lax.axis_size(axis))
    route = [((i - distance) % len(devices), i) for i in devices]
    return lax.ppermute(block, axis, route)


def advance(state_now, conv_mats, gain_row, first_proj, second_proj):
    members, channels, lat_rows, lon_cols = state_now.shape
    padded = with_halo(state_now, (("space", 2),), 1)
    summed = jnp.zeros((members, channels, lat_rows * lon_cols), jnp.float32)
    for lat_step in range(3):
        band_rows = padded[:, :, lat_step : lat_step + lat_rows, :]
        for lon_step in range(3):
            shifted = jnp.roll(band_rows, 1 - lon_step, axis=3).reshape(
                members, channels, lat_rows * lon_cols
            )
            summed = summed + jnp.einsum(
                "oi,mip->mop",
                conv_mats[3 * lat_step + lon_step],
                shifted,
                preferred_element_type=jnp.float32,
            )
    updated = state_now.reshape(members, channels, lat_rows * lon_cols).astype(jnp.float32) + summed
    normed = (
        updated
        * lax.rsqrt(jnp.mean(updated * updated, axis=1, keepdims=True) + EPSILON)
        * gain_row[None, :, None]
    ).astype(jnp.bfloat16)
    hidden = jax.nn.silu(
        jnp.einsum("hc,mcp->mhp", first_proj, normed, preferred_element_type=jnp.float32)
    ).astype(jnp.bfloat16)
    result = updated + jnp.einsum(
        "ch,mhp->mcp", second_proj, hidden, preferred_element_type=jnp.float32
    )
    return result.astype(jnp.bfloat16).reshape(members, channels, lat_rows, lon_cols)


def sample_tile(tile_data, points_row, channel_row):
    flat_tile = tile_data.reshape(tile_data.shape[0], -1)
    return flat_tile[:, channel_row * tile_data.shape[2] + points_row].astype(jnp.float32)


def prepare(sampled, value_row, precision_row, live_count):
    average = jnp.mean(sampled, axis=0)
    spread = sampled - average
    slots = jnp.arange(value_row.shape[0], dtype=jnp.int32)
    weight_matrix = jnp.where(slots < live_count, precision_row, jnp.zeros_like(precision_row))
    return (spread, weight_matrix, value_row - average)


def moments(spread, weight_matrix, innovation):
    gram = jnp.dot(spread * weight_matrix[None, :], spread.T, precision=HIGHEST_PRECISION)
    vector = jnp.dot(spread, weight_matrix * innovation, precision=HIGHEST_PRECISION)
    return (gram, vector)


def transform(gram, vector):
    sample_collection = gram.shape[0]
    identity = jnp.eye(sample_collection, dtype=jnp.float32)
    system = (sample_collection - 1.0) * identity + gram
    scale = jnp.sqrt(jnp.sum(system * system))
    root = system / scale
    inverse = identity
    for sweep_index in range(NS_STEPS):
        middle = 0.5 * (3.0 * identity - jnp.dot(inverse, root, precision=HIGHEST_PRECISION))
        root, inverse = (
            jnp.dot(root, middle, precision=HIGHEST_PRECISION),
            jnp.dot(middle, inverse, precision=HIGHEST_PRECISION),
        )
    covariance = jnp.dot(inverse, inverse, precision=HIGHEST_PRECISION) / scale
    mean_weight = jnp.dot(covariance, vector, precision=HIGHEST_PRECISION)
    full = jnp.sqrt((sample_collection - 1.0) / scale) * inverse + mean_weight[:, None]
    return (full + (1.0 - jnp.sum(full, axis=0, keepdims=True)) / sample_collection).astype(
        jnp.bfloat16
    )


def blend(tile_data, mixing):
    return jnp.einsum("kcp,kl->lcp", tile_data, mixing, preferred_element_type=jnp.float32).astype(
        jnp.bfloat16
    )


def fetch_rows(spread, weight_matrix, innovation, offset):
    return shifted_2((spread, weight_matrix, innovation), "member", offset)


def weights_for(sampled, value_row, precision_row, live_count):
    spread, weight_matrix, innovation = prepare(sampled, value_row, precision_row, live_count)
    before = fetch_rows(spread, weight_matrix, innovation, 1)
    after = fetch_rows(spread, weight_matrix, innovation, -1)
    spread_total = jnp.concatenate([spread, before[0], after[0]], axis=1)
    weight_all = jnp.concatenate([weight_matrix, NEAR_WEIGHT * before[1], NEAR_WEIGHT * after[1]])
    innovation_all = jnp.concatenate([innovation, before[2], after[2]])
    gram, vector = moments(spread_total, weight_all, innovation_all)
    return transform(gram, vector)


def body(
    starting_fields,
    conv_weight,
    norm_gain,
    weight_in,
    weight_out,
    obs_count,
    obs_point,
    obs_channel,
    obs_value,
    obs_precision,
):
    state_now = starting_fields
    state_now = advance(state_now, conv_weight[0], norm_gain[0], weight_in[0], weight_out[0])
    local_members, channels, lat_rows, lon_cols = state_now.shape
    band_points = lat_rows * lon_cols
    flat_state = state_now.reshape(local_members, channels, band_points)
    live_count = obs_count[0, 0]
    value_row = obs_value[0, 0]
    precision_row = obs_precision[0, 0]
    tile_data = lax.all_to_all(flat_state, "member", split_axis=2, concat_axis=0, tiled=True)
    sampled = sample_tile(tile_data, obs_point[0, 0], obs_channel[0, 0])
    mixing = weights_for(sampled, value_row, precision_row, live_count)
    analysed = lax.all_to_all(
        blend(tile_data, mixing), "member", split_axis=0, concat_axis=2, tiled=True
    )
    return analysed.reshape(local_members, channels, lat_rows, lon_cols)


def solution(mesh):
    in_specs = (
        P("member", None, "space", None),
        P(),
        P(),
        P(),
        P(),
        P("space", "member"),
        P("space", "member", None),
        P("space", "member", None),
        P("space", "member", None),
        P("space", "member", None),
    )
    out_specs = P("member", None, "space", None)
    return jax.shard_map(body, mesh=mesh, in_specs=in_specs, out_specs=out_specs, check_vma=False)
```

profile of v0, /device:TPU:2, one launch (start us, length us, event | category | flops | bytes accessed | tf_op | source)
XLA Modules:
  0.0 132.6 jit_solution(2541110111980543657)
XLA Ops:
  0.0 1.8 %fusion.65 = (bf16[2,80,1,360]{3,2,1,0:T(2,128)(2,1)S(1)}, bf16[2,80,1,360]{3,2,1,0:T(2,128)(2,1)S(1)}) fusion(bf16[2,80,4,360]{3,2,1,0:T(4,128)(2,1)} %param.10), kind=kLoop, calls=%fused_computation.122 | loop fusion | bytes 460800 | tf_op jit(solution)/shard_map/slice | solution.py:22
  1.8 1.9 %collective-permute-start = (bf16[2,80,1,360]{3,2,1,0:T(2,128)(2,1)S(1)}, bf16[2,80,1,360]{3,2,1,0:T(2,128)(2,1)S(1)}, u32[]{:S(2)}, u32[]{:S(2)}) collective-permute-start(bf16[2,80,1,360]{3,2,1,0:T(2,128)(2,1)S(1)} %get-tuple-element.23), channel_id=1, source_target_pairs={{0,1},{1,2},{2,3},{3,4},{4,5},{5,6},{6,7},{8,9},{9,10},{10,11},{11... | collective-permute-start | bytes 345608 | tf_op jit(solution)/shard_map/ppermute | solution.py:19
  3.7 3.6 %collective-permute-start.1 = (bf16[2,80,1,360]{3,2,1,0:T(2,128)(2,1)S(1)}, bf16[2,80,1,360]{3,2,1,0:T(2,128)(2,1)S(1)}, u32[]{:S(2)}, u32[]{:S(2)}) collective-permute-start(bf16[2,80,1,360]{3,2,1,0:T(2,128)(2,1)S(1)} %get-tuple-element.22), channel_id=1, source_target_pairs={{1,0},{2,1},{3,2},{4,3},{5,4},{6,5},{7,6},{9,8},{10,9},{11,10},{12... | collective-permute-start | bytes 345608 | tf_op jit(solution)/shard_map/ppermute | solution.py:22
  7.3 1.9 %fusion.66 = (bf16[2,80,4,1]{3,2,1,0:T(4,128)(2,1)}, bf16[2,80,4,1]{3,2,1,0:T(4,128)(2,1)}) fusion(bf16[2,80,4,360]{3,2,1,0:T(4,128)(2,1)} %param.10), kind=kLoop, calls=%fused_computation.123 | loop fusion | bytes 5120 | tf_op jit(solution)/shard_map/jit(_roll_static)/slice | solution.py:40
  11.0 3.7 %fusion.15 = (bf16[2,80,4,359]{3,2,1,0:T(4,128)(2,1)S(1)}, bf16[2,80,4,359]{3,2,1,0:T(4,128)(2,1)S(1)}, bf16[2,80,4,359]{3,2,1,0:T(4,128)(2,1)S(1)}, bf16[2,80,4...) fusion(bf16[2,80,4,360]{3,2,1,0:T(4,128)(2,1)S(1)} %copy-done.1, ...), kind=kLoop, calls=%fused_computation.52 | loop fusion | flops 3676160 | bytes 4723200 | tf_op jit(solution)/shard_map/concatenate | solution.py:23
  14.7 6.1 %fusion.21 = (bf16[2,80,4,360]{3,2,1,0:T(4,128)(2,1)}, bf16[2,80,4,360]{3,2,1,0:T(4,128)(2,1)}, bf16[2,80,4,360]{3,2,1,0:T(4,128)(2,1)S(1)}, bf16[2,80,4,360]{3,...) fusion(bf16[2,80,1,360]{3,2,1,0:T(2,128)(2,1)} %copy-done.5, ...), kind=kLoop, calls=%fused_computation.59 | loop fusion | flops 7372800 | bytes 5294080 | tf_op jit(solution)/shard_map/jit(_roll_static)/concatenate | solution.py:40
  20.8 2.3 %reshape.108 = bf16[2,80,1440]{2,1,0:T(8,128)(2,1)} reshape(bf16[2,80,4,360]{3,2,1,0:T(4,128)(2,1)} %get-tuple-element.16) | data formatting | bytes 921600 | tf_op jit(solution)/shard_map/reshape | solution.py:40
  23.8 2.6 %pad_maximum_fusion.4 = (bf16[2,80,4,360]{3,2,1,0:T(4,128)(2,1)}, bf16[2,80,4,360]{3,2,1,0:T(4,128)(2,1)S(1)}) fusion(bf16[2,80,4,359]{3,2,1,0:T(4,128)(2,1)S(1)} %get-tuple-element.19, bf16[2,80,4,1]{3,2,1,0:T(4,128)(2,1)} %get-tuple-element.25, bf16[2,80,4,1]{3,2,1,0:T(4,128)(2,1)} %get-tuple-element.24, bf16[2,80,4,359]{3,2,1,0:T(4,128)(2,1)S(1)} %get-tuple-element.18), kind=kLoop, calls=%fused_computation.66 | loop fusion | flops 1843200 | bytes 1843200 | tf_op jit(solution)/shard_map/jit(_roll_static)/concatenate | solution.py:40
  28.5 1.4 %reshape.113 = bf16[2,80,1440]{2,1,0:T(8,128)(2,1)S(1)} reshape(bf16[2,80,4,360]{3,2,1,0:T(4,128)(2,1)} %get-tuple-element.6) | data formatting | bytes 921600 | tf_op jit(solution)/shard_map/reshape | solution.py:40
  30.0 2.2 %reshape.114 = bf16[2,80,1440]{2,1,0:T(8,128)(2,1)} reshape(bf16[2,80,4,360]{3,2,1,0:T(4,128)(2,1)} %get-tuple-element.5) | data formatting | bytes 921600 | tf_op jit(solution)/shard_map/reshape | solution.py:40
  37.0 1.7 %fusion.7 = bf16[2,80,1440]{2,1,0:T(8,128)(2,1)S(1)} fusion(f32[2,80,1440]{2,1,0:T(8,128)S(1)} %get-tuple-element.31, f32[80]{0:T(128)S(1)} %bitcast.162, f32[2,1440]{1,0:T(2,128)S(1)} %add_rsqrt_fusion, bf16[1,80,320]{2,1,0:T(8,128)(2,1)S(1)} %copy-done, bf16[1,320,80]{1,2,0:T(8,128)(2,1)S(1)} %copy-done.11), kind=kOutput, calls=%fused_computation.19 | convolution fusion | flops 300672000 | bytes 1496640 | tf_op jit(solution)/shard_map/ch,mhp->mcp/dot_general | solution.py:58
  38.7 1.8 %copy.22 = bf16[2,80,1440]{1,0,2:T(2,128)(2,1)} copy(bf16[2,80,1440]{2,1,0:T(8,128)(2,1)S(1)} %fusion.7) | data formatting | bytes 921600 | tf_op jit(solution)/shard_map/convert_element_type | solution.py:61
  40.5 11.7 %all-to-all-start = ((bf16[2,80,1440]{1,0,2:T(2,128)(2,1)}), bf16[2,80,1440]{1,0,2:T(2,128)(2,1)S(1)}, u32[]{:S(2)}, u32[]{:S(2)}) async-start(bf16[2,80,1440]{1,0,2:T(2,128)(2,1)} %copy.22), calls=%async_computation | async-start | bytes 1474560 | tf_op jit(solution)/shard_map/all_to_all | solution.py:145
  52.2 5.3 %collective-permute-start.5 = (f32[256]{0:T(256)S(1)}, f32[256]{0:T(256)S(1)}, u32[]{:S(2)}, u32[]{:S(2)}) collective-permute-start(f32[256]{0:T(256)S(1)} %compare_select_fusion.1), channel_id=1, source_target_pairs={{8,0},{16,8},{24,16},{32,24},{40,32},{48,40},{56,48},{64,56},{72,6... | collective-permute-start | bytes 3080 | tf_op jit(solution)/shard_map/ppermute | solution.py:30
  57.5 13.0 %collective-permute-done.5 = f32[256]{0:T(256)S(1)} collective-permute-done((f32[256]{0:T(256)S(1)}, f32[256]{0:T(256)S(1)}, u32[]{:S(2)}, u32[]{:S(2)}) %collective-permute-start.5) | collective-permute-done | bytes 1056 | tf_op jit(solution)/shard_map/ppermute | solution.py:30
  71.0 2.3 %all-to-all-done = bf16[2,80,1440]{1,0,2:T(2,128)(2,1)S(1)} async-done(((bf16[2,80,1440]{1,0,2:T(2,128)(2,1)}), bf16[2,80,1440]{1,0,2:T(2,128)(2,1)S(1)}, u32[]{:S(2)}, u32[]{:S(2)}) %all-to-all-start) | async-done | bytes 460832 | tf_op jit(solution)/shard_map/all_to_all | solution.py:145
  73.3 2.3 %copy.23 = bf16[32,2,80,45]{3,2,1,0:T(8,128)(2,1)S(1)} copy(bf16[32,2,80,45]{2,1,3,0:T(2,128)(2,1)S(1)} %bitcast.154) | data formatting | bytes 921600 | tf_op jit(solution)/shard_map/all_to_all | solution.py:145
  78.3 3.7 %collective-permute-start.6 = (f32[256]{0:T(256)S(1)}, f32[256]{0:T(256)S(1)}, u32[]{:S(2)}, u32[]{:S(2)}) collective-permute-start(f32[256]{0:T(256)S(1)} %get-tuple-element.28), channel_id=1, source_target_pairs={{248,0},{0,8},{8,16},{16,24},{24,32},{32,40},{40,48},{48,56},{56,6... | collective-permute-start | bytes 3080 | tf_op jit(solution)/shard_map/ppermute | solution.py:30
  82.0 1.7 %collective-permute-start.7 = (f32[256]{0:T(256)S(1)}, f32[256]{0:T(256)S(1)}, u32[]{:S(2)}, u32[]{:S(2)}) collective-permute-start(f32[256]{0:T(256)S(1)} %get-tuple-element.28), channel_id=1, source_target_pairs={{8,0},{16,8},{24,16},{32,24},{40,32},{48,40},{56,48},{64,56},{72,6... | collective-permute-start | bytes 3080 | tf_op jit(solution)/shard_map/ppermute | solution.py:30
  84.2 5.0 %collective-permute-start.3 = (f32[64,256]{0,1:T(8,128)S(1)}, f32[64,256]{0,1:T(8,128)S(1)}, u32[]{:S(2)}, u32[]{:S(2)}) collective-permute-start(f32[64,256]{0,1:T(8,128)S(1)} %fusion.30), channel_id=1, source_target_pairs={{8,0},{16,8},{24,16},{32,24},{40,32},{48,40},{56,48},{64,56},{72,6... | collective-permute-start | bytes 196616 | tf_op jit(solution)/shard_map/ppermute | solution.py:30
  90.1 3.4 %collective-permute-done.2 = f32[64,256]{0,1:T(8,128)S(1)} collective-permute-done((f32[64,256]{0,1:T(8,128)S(1)}, f32[64,256]{0,1:T(8,128)S(1)}, u32[]{:S(2)}, u32[]{:S(2)}) %collective-permute-start.2) | collective-permute-done | bytes 65568 | tf_op jit(solution)/shard_map/ppermute | solution.py:30
  93.5 1.5 %multiply_reduce_fusion.1 = (f32[]{:T(128)}, f32[64,64]{1,0:T(8,128)S(1)}) fusion(f32[64,256]{0,1:T(8,128)S(1)} %collective-permute-done.3, f32[64,256]{0,1:T(8,128)S(1)} %collective-permute-done.2, f32[64,256]{0,1:T(8,128)S(1)} %fusion.30, f32[768]{0:T(1024)S(1)} %get-tuple-element.27), kind=kOutput, calls=%fused_computation.79 | convolution fusion | flops 38014976 | bytes 216068 | tf_op jit(solution)/shard_map/dot_general | solution.py:78
  100.4 29.9 %all_to_all.33 = bf16[64,80,45]{1,2,0:T(8,128)(2,1)S(1)} all-to-all(bf16[64,80,45]{1,2,0:T(8,128)(2,1)S(1)} %copy.27), channel_id=1, replica_groups=mesh['member'=32,'space'=8] {'member'}, dimensions={0} | all-to-all | bytes 921600 | tf_op jit(solution)/shard_map/all_to_all | solution.py:148
  130.8 1.8 %copy.29 = bf16[2,80,4,360]{3,2,1,0:T(4,128)(2,1)} copy(bf16[2,80,4,360]{1,0,3,2:T(2,128)(2,1)S(1)} %bitcast.158) | data formatting | bytes 921600 | tf_op jit(solution)/shard_map/reshape | solution.py:151
  (89 shorter events, 18.2 us)
Async XLA Ops:
  0.0 36.6 %copy-start = (bf16[1,80,320]{2,1,0:T(8,128)(2,1)S(1)}, bf16[1,80,320]{2,1,0:T(8,128)(2,1)}, u32[]{:S(2)}) copy-start(bf16[1,80,320]{2,1,0:T(8,128)(2,1)} %param.14) | copy-start | bytes 153604
  0.0 9.2 %copy-start.1 = (bf16[2,80,4,360]{3,2,1,0:T(4,128)(2,1)S(1)}, bf16[2,80,4,360]{3,2,1,0:T(4,128)(2,1)}, u32[]{:S(2)}) copy-start(bf16[2,80,4,360]{3,2,1,0:T(4,128)(2,1)} %param.10) | copy-start | bytes 1382404
  1.8 8.5 %collective-permute-start = (bf16[2,80,1,360]{3,2,1,0:T(2,128)(2,1)S(1)}, bf16[2,80,1,360]{3,2,1,0:T(2,128)(2,1)S(1)}, u32[]{:S(2)}, u32[]{:S(2)}) collective-permute-start(bf16[2,80,1,360]{3,2,1,0:T(2,128)(2,1)S(1)} %get-tuple-element.23), channel_id=1, source_target_pairs={{0,1},{1,2},{2,3},{3,4},{4,5},{5,6},{6,7},{8,9},{9,10},{10,11},{11... | collective-permute-start | bytes 345608 | tf_op jit(solution)/shard_map/ppermute | solution.py:19
  3.7 7.3 %collective-permute-start.1 = (bf16[2,80,1,360]{3,2,1,0:T(2,128)(2,1)S(1)}, bf16[2,80,1,360]{3,2,1,0:T(2,128)(2,1)S(1)}, u32[]{:S(2)}, u32[]{:S(2)}) collective-permute-start(bf16[2,80,1,360]{3,2,1,0:T(2,128)(2,1)S(1)} %get-tuple-element.22), channel_id=1, source_target_pairs={{1,0},{2,1},{3,2},{4,3},{5,4},{6,5},{7,6},{9,8},{10,9},{11,10},{12... | collective-permute-start | bytes 345608 | tf_op jit(solution)/shard_map/ppermute | solution.py:22
  10.2 4.5 %copy-start.4 = (bf16[2,80,1,360]{3,2,1,0:T(2,128)(2,1)}, bf16[2,80,1,360]{3,2,1,0:T(2,128)(2,1)S(1)}, u32[]{:S(2)}) copy-start(bf16[2,80,1,360]{3,2,1,0:T(2,128)(2,1)S(1)} %collective-permute-done) | copy-start | bytes 345604
  11.0 3.7 %copy-start.5 = (bf16[2,80,1,360]{3,2,1,0:T(2,128)(2,1)}, bf16[2,80,1,360]{3,2,1,0:T(2,128)(2,1)S(1)}, u32[]{:S(2)}) copy-start(bf16[2,80,1,360]{3,2,1,0:T(2,128)(2,1)S(1)} %collective-permute-done.1) | copy-start | bytes 345604
  20.8 2.3 %copy-start.3 = (bf16[2,80,4,360]{3,2,1,0:T(4,128)(2,1)S(1)}, bf16[2,80,4,360]{3,2,1,0:T(4,128)(2,1)}, u32[]{:S(2)}) copy-start(bf16[2,80,4,360]{3,2,1,0:T(4,128)(2,1)} %get-tuple-element.15) | copy-start | bytes 1382404
  32.2 1.3 %copy-start.6 = (bf16[1,9,80,80]{3,2,1,0:T(8,128)(2,1)S(1)}, bf16[1,9,80,80]{3,2,1,0:T(8,128)(2,1)}, u32[]{:S(2)}) copy-start(bf16[1,9,80,80]{3,2,1,0:T(8,128)(2,1)} %param.11) | copy-start | bytes 345604
  35.1 1.0 copy-start.2
  36.2 0.8 copy-start.11
  36.2 0.8 copy-start.12
  38.7 13.5 %copy-start.9 = (f32[1,1,256]{2,1,0:T(1,128)S(1)}, f32[1,1,256]{2,1,0:T(1,128)}, u32[]{:S(2)}) copy-start(f32[1,1,256]{2,1,0:T(1,128)} %param.19) | copy-start | bytes 3076
  38.7 18.8 %copy-start.7 = (s32[1,1,256]{2,1,0:T(1,128)S(1)}, s32[1,1,256]{2,1,0:T(1,128)}, u32[]{:S(2)}) copy-start(s32[1,1,256]{2,1,0:T(1,128)} %param.16) | copy-start | bytes 3076
  38.7 18.8 %copy-start.8 = (s32[1,1,256]{2,1,0:T(1,128)S(1)}, s32[1,1,256]{2,1,0:T(1,128)}, u32[]{:S(2)}) copy-start(s32[1,1,256]{2,1,0:T(1,128)} %param.17) | copy-start | bytes 3076
  40.5 32.8 %all-to-all-start = ((bf16[2,80,1440]{1,0,2:T(2,128)(2,1)}), bf16[2,80,1440]{1,0,2:T(2,128)(2,1)S(1)}, u32[]{:S(2)}, u32[]{:S(2)}) async-start(bf16[2,80,1440]{1,0,2:T(2,128)(2,1)} %copy.22), calls=%async_computation | async-start | bytes 1474560 | tf_op jit(solution)/shard_map/all_to_all | solution.py:145
  52.2 18.3 %collective-permute-start.5 = (f32[256]{0:T(256)S(1)}, f32[256]{0:T(256)S(1)}, u32[]{:S(2)}, u32[]{:S(2)}) collective-permute-start(f32[256]{0:T(256)S(1)} %compare_select_fusion.1), channel_id=1, source_target_pairs={{8,0},{16,8},{24,16},{32,24},{40,32},{48,40},{56,48},{64,56},{72,6... | collective-permute-start | bytes 3080 | tf_op jit(solution)/shard_map/ppermute | solution.py:30
  57.5 13.5 %collective-permute-start.4 = (f32[256]{0:T(256)S(1)}, f32[256]{0:T(256)S(1)}, u32[]{:S(2)}, u32[]{:S(2)}) collective-permute-start(f32[256]{0:T(256)S(1)} %compare_select_fusion.1), channel_id=1, source_target_pairs={{248,0},{0,8},{8,16},{16,24},{24,32},{32,40},{40,48},{48,56},{56,6... | collective-permute-start | bytes 3080 | tf_op jit(solution)/shard_map/ppermute | solution.py:30
  76.8 1.4 %copy-start.10 = (f32[1,1,256]{2,1,0:T(1,128)S(1)}, f32[1,1,256]{2,1,0:T(1,128)}, u32[]{:S(2)}) copy-start(f32[1,1,256]{2,1,0:T(1,128)} %param.18) | copy-start | bytes 3076
  78.3 11.7 %collective-permute-start.6 = (f32[256]{0:T(256)S(1)}, f32[256]{0:T(256)S(1)}, u32[]{:S(2)}, u32[]{:S(2)}) collective-permute-start(f32[256]{0:T(256)S(1)} %get-tuple-element.28), channel_id=1, source_target_pairs={{248,0},{0,8},{8,16},{16,24},{24,32},{32,40},{40,48},{48,56},{56,6... | collective-permute-start | bytes 3080 | tf_op jit(solution)/shard_map/ppermute | solution.py:30
  82.0 8.0 %collective-permute-start.7 = (f32[256]{0:T(256)S(1)}, f32[256]{0:T(256)S(1)}, u32[]{:S(2)}, u32[]{:S(2)}) collective-permute-start(f32[256]{0:T(256)S(1)} %get-tuple-element.28), channel_id=1, source_target_pairs={{8,0},{16,8},{24,16},{32,24},{40,32},{48,40},{56,48},{64,56},{72,6... | collective-permute-start | bytes 3080 | tf_op jit(solution)/shard_map/ppermute | solution.py:30
  83.8 9.6 %collective-permute-start.2 = (f32[64,256]{0,1:T(8,128)S(1)}, f32[64,256]{0,1:T(8,128)S(1)}, u32[]{:S(2)}, u32[]{:S(2)}) collective-permute-start(f32[64,256]{0,1:T(8,128)S(1)} %fusion.30), channel_id=1, source_target_pairs={{248,0},{0,8},{8,16},{16,24},{24,32},{32,40},{40,48},{48,56},{56,6... | collective-permute-start | bytes 196616 | tf_op jit(solution)/shard_map/ppermute | solution.py:30
  84.2 9.3 %collective-permute-start.3 = (f32[64,256]{0,1:T(8,128)S(1)}, f32[64,256]{0,1:T(8,128)S(1)}, u32[]{:S(2)}, u32[]{:S(2)}) collective-permute-start(f32[64,256]{0,1:T(8,128)S(1)} %fusion.30), channel_id=1, source_target_pairs={{8,0},{16,8},{24,16},{32,24},{40,32},{48,40},{56,48},{64,56},{72,6... | collective-permute-start | bytes 196616 | tf_op jit(solution)/shard_map/ppermute | solution.py:30
where the time goes:
time: 133 us
  starting transfers between devices  33.4 us (25%)
  blocking collectives  29.9 us (22%)
  local copies, waits for them, and re-layouts  24.2 us (18%)
  waiting for transfers between devices  20 us (15%)
  other arithmetic  12.7 us (10%)
  matrix products  10.6 us (8%)
  between operations  1.97 us (1%)
    all_to_all x1, blocking collectives, body(): lax.all_to_all(blend(tile_data, mixing), 'member', split_axis=0, concat_a...  29.9 us
    ppermute x6, waiting for transfers between devices, shifted_2(): return lax.ppermute(block, axis, route)  16.9 us
    ppermute x6, starting transfers between devices, shifted_2(): return lax.ppermute(block, axis, route)  16.1 us
    all_to_all x1, starting transfers between devices, body(): lax.all_to_all(flat_state, 'member', split_axis=2, concat_axis=0, tiled=T...  11.7 us
    reshape x8, local copies, waits for them, and re-layouts, advance(): jnp.roll(band_rows, 1 - lon_step, axis=3)  8.76 us
    concatenate x2, other arithmetic, advance(): jnp.roll(band_rows, 1 - lon_step, axis=3)  8.64 us
    concatenate x1, other arithmetic, with_halo(): block = jnp.concatenate([low, block, high], axis=dim)  3.67 us
    ppermute x1, starting transfers between devices, with_halo(): lax.ppermute(lax.slice_in_dim(block, 0, width, axis=dim), axis, backward)  3.64 us
  transfers between devices with their start and end apart: 9, of which 5 were waited for; matrix products, arithmetic and copies ran while one was open for 2% of the time, Pallas kernels for 0%

commit v1 on v0

v1 whole, which is shorter than its diff:
```python
import jax
import jax.numpy as jnp
from jax import lax
from jax.experimental import pallas as pl
from jax.experimental.pallas import tpu as pltpu
from jax.sharding import PartitionSpec as P

NS_STEPS = 6
NEAR_WEIGHT = 0.5
EPSILON = 1e-06
MEMBERS = 64
CHANNELS = 80
ROWS = 4
LON = 360
WIDE = 384
POINTS = 45
TILES = 32
PER_ROW = 8
SUB = 8
SLOTS = CHANNELS // SUB
PACK = 512
OBS = 256
HID = 320

F32 = jnp.float32
BF16 = jnp.bfloat16


def mm(left, right):
    return jnp.dot(left, right, preferred_element_type=F32)


def mm_t(left, right):
    return lax.dot_general(left, right, (((1,), (1,)), ((), ())), preferred_element_type=F32)


def halves(value):
    high = value.astype(BF16)
    return high, (value - high.astype(F32)).astype(BF16)


def mm_split(left, right, product=mm):
    left_high, left_low = halves(left)
    right_high, right_low = halves(right)
    return product(left_high, right_high) + (
        product(left_high, right_low) + product(left_low, right_high)
    )


def pieces(source, target, length):
    found = []
    done = 0
    while done < length:
        a, b = source + done, target + done
        step = min(length - done, 128 - a % 128, 128 - b % 128)
        found.append((a // 128, b // 128, (b - a) % 128, b % 128, b % 128 + step))
        done += step
    return found


def move(value, shift):
    return pltpu.roll(value, shift, 1) if shift else value


def forecast_kernel(x_ref, low_ref, high_ref, conv_ref, gain_ref, first_ref, second_ref, out_ref, held):
    conv = jnp.concatenate(
        [conv_ref[0, 3 * a : 3 * a + 3].reshape(3 * CHANNELS, CHANNELS) for a in range(3)], axis=1
    )
    first = first_ref[0]
    second = second_ref[0]
    gain = gain_ref[...]
    lane = lax.broadcasted_iota(jnp.int32, (CHANNELS, 128), 1)

    def row(m, r):
        if r < 0:
            return low_ref[m]
        if r >= ROWS:
            return high_ref[m]
        return x_ref[m, r]

    for m in range(2):
        for h in range(2):
            rows = [row(m, 2 * h + d) for d in range(-1, 3)]
            stacked = jnp.concatenate(
                [jnp.concatenate([rows[a], rows[a + 1]], axis=1) for a in range(3)], axis=0
            )
            taps = mm(conv, stacked)
            parts = []
            for d in range(2):
                at = WIDE * d
                west = taps[:CHANNELS, at : at + WIDE]
                here = taps[CHANNELS : 2 * CHANNELS, at : at + WIDE]
                east = taps[2 * CHANNELS :, at : at + WIDE]
                end = (LON - 1) % 128
                first_wrap = move(west[:, 256:], 128 - end)
                last_wrap = move(east[:, :128], end)
                west = pltpu.roll(west, 1, 1)
                east = pltpu.roll(east, WIDE - 1, 1)
                west = jnp.concatenate([jnp.where(lane == 0, first_wrap, west[:, :128]), west[:, 128:]], axis=1)
                east = jnp.concatenate([east[:, :256], jnp.where(lane == end, last_wrap, east[:, 256:])], axis=1)
                parts.append(rows[d + 1].astype(F32) + (here + west + east))
            updated = jnp.concatenate(parts, axis=1)
            power = jnp.sum(updated * updated, axis=0, keepdims=True) * (1.0 / CHANNELS)
            normed = (updated * lax.rsqrt(power + EPSILON) * gain).astype(BF16)
            hidden = mm(first, normed)
            hidden = (hidden * (0.5 + 0.5 * jnp.tanh(0.5 * hidden))).astype(BF16)
            result = updated + mm(second, hidden)
            held[2 * h, m] = result[:, :WIDE]
            held[2 * h + 1, m] = result[:, WIDE:]

    spot = lax.broadcasted_iota(jnp.int32, (2 * SUB, 128), 1)

    @pl.loop(0, ROWS)
    def _(r):
        for j in range(PER_ROW):
            packed = [jnp.zeros((2 * SUB, 128), F32) for _ in range(PACK // 128)]
            for s in range(SLOTS):
                for a, b, shift, start, stop in pieces(j * POINTS, s * POINTS, POINTS):
                    both = held[r, :, s * SUB : (s + 1) * SUB, a * 128 : (a + 1) * 128]
                    both = move(both.reshape(2 * SUB, 128), shift)
                    packed[b] = jnp.where((spot >= start) & (spot < stop), both, packed[b])
            at = pl.multiple_of((r * PER_ROW + j) * 2 * SUB, 2 * SUB)
            out_ref[pl.ds(at, 2 * SUB), :] = jnp.concatenate(packed, axis=1).astype(BF16)


def observe_kernel(count_ref, tile_ref, point_ref, channel_ref, value_ref, precision_ref, out_ref):
    channel = channel_ref[...]
    lane = (channel // SUB) * POINTS + point_ref[...]
    place = lax.broadcasted_iota(jnp.int32, (PACK, OBS), 0)
    chosen = jnp.where(place == lane, 1.0, 0.0).astype(BF16)
    found = mm(tile_ref[...], chosen)
    found = jnp.where(place % SUB == channel % SUB, found, 0.0)
    sampled = jnp.sum(found.reshape(MEMBERS, SUB, OBS), axis=1)
    average = jnp.sum(sampled, axis=0, keepdims=True) * (1.0 / MEMBERS)
    spread = sampled - average
    slots = lax.broadcasted_iota(jnp.int32, (1, OBS), 1)
    weight = jnp.where(slots < count_ref[0, 0], precision_ref[...], 0.0)
    innovation = value_ref[...] - average
    out_ref[:, :MEMBERS] = mm_split(spread * weight, spread, mm_t)
    out_ref[:, MEMBERS : MEMBERS + 1] = jnp.sum(spread * (weight * innovation), axis=1, keepdims=True)
    out_ref[:, MEMBERS + 1 :] = jnp.zeros((MEMBERS, 128 - MEMBERS - 1), F32)


def blend_kernel(own_ref, before_ref, after_ref, tile_ref, out_ref):
    total = own_ref[...] + NEAR_WEIGHT * (before_ref[...] + after_ref[...])
    gram = total[:, :MEMBERS]
    vector = total[:, MEMBERS : MEMBERS + 1]
    identity = jnp.where(
        lax.broadcasted_iota(jnp.int32, (MEMBERS, MEMBERS), 0)
        == lax.broadcasted_iota(jnp.int32, (MEMBERS, MEMBERS), 1),
        1.0,
        0.0,
    )
    system = (MEMBERS - 1.0) * identity + gram
    squares = jnp.sum(jnp.sum(system * system, axis=0, keepdims=True), axis=1, keepdims=True)
    scale = jnp.sqrt(squares)
    root = system / scale
    middle = 1.5 * identity - 0.5 * root
    root = mm_split(root, middle)
    inverse = middle
    for sweep in range(1, NS_STEPS):
        middle = 1.5 * identity - 0.5 * mm_split(inverse, root)
        if sweep < NS_STEPS - 1:
            root = mm_split(root, middle)
        inverse = mm_split(middle, inverse)
    covariance = mm_split(inverse, inverse) / scale
    mean_weight = jnp.sum(covariance * vector, axis=0, keepdims=True)
    full = jnp.sqrt((MEMBERS - 1.0) / scale) * inverse + mean_weight
    mixing = full + (1.0 - jnp.sum(full, axis=1, keepdims=True)) * (1.0 / MEMBERS)
    mixing = mixing.astype(BF16)
    spread_rows = jnp.where(
        lax.broadcasted_iota(jnp.int32, (PACK, MEMBERS), 0) // SUB
        == lax.broadcasted_iota(jnp.int32, (PACK, MEMBERS), 1),
        1.0,
        0.0,
    ).astype(BF16)
    spread_cols = jnp.where(
        lax.broadcasted_iota(jnp.int32, (MEMBERS, PACK), 1) // SUB
        == lax.broadcasted_iota(jnp.int32, (MEMBERS, PACK), 0),
        1.0,
        0.0,
    ).astype(BF16)
    tall = mm(spread_rows, mixing).astype(BF16)
    square = mm(tall, spread_cols)
    same = (
        lax.broadcasted_iota(jnp.int32, (PACK, PACK), 0) % SUB
        == lax.broadcasted_iota(jnp.int32, (PACK, PACK), 1) % SUB
    )
    square = jnp.where(same, square, 0.0).astype(BF16)
    out_ref[...] = mm(square, tile_ref[...]).astype(BF16)


def unpack_kernel(in_ref, out_ref):
    spot = lax.broadcasted_iota(jnp.int32, (2 * SUB, 128), 1)

    @pl.loop(0, ROWS)
    def _(r):
        for pair in range(SLOTS // 2):
            lines = []
            for s in (2 * pair, 2 * pair + 1):
                line = [jnp.zeros((2 * SUB, 128), F32) for _ in range(WIDE // 128)]
                for j in range(PER_ROW):
                    at = pl.multiple_of((r * PER_ROW + j) * 2 * SUB, 2 * SUB)
                    for a, b, shift, start, stop in pieces(s * POINTS, j * POINTS, POINTS):
                        both = in_ref[pl.ds(at, 2 * SUB), a * 128 : (a + 1) * 128].astype(F32)
                        line[b] = jnp.where((spot >= start) & (spot < stop), move(both, shift), line[b])
                lines.append(jnp.concatenate(line, axis=1))
            for m in range(2):
                joined = jnp.concatenate([line[m * SUB : (m + 1) * SUB] for line in lines], axis=0)
                out_ref[m, r, pair * 2 * SUB : (pair + 1) * 2 * SUB, :] = joined.astype(BF16)[:, :LON]


def call(kernel, out_shape, *operands, **more):
    return pl.pallas_call(
        kernel,
        out_shape=out_shape,
        compiler_params=pltpu.CompilerParams(vmem_limit_bytes=40 * 1024 * 1024),
        **more,
    )(*operands)


def body(
    starting_fields,
    conv_weight,
    norm_gain,
    weight_in,
    weight_out,
    obs_count,
    obs_point,
    obs_channel,
    obs_value,
    obs_precision,
):
    fields = jnp.pad(starting_fields.transpose(0, 2, 1, 3), ((0, 0), (0, 0), (0, 0), (0, WIDE - LON)))
    bands = lax.axis_size("space")
    north = [(i, i + 1) for i in range(bands - 1)]
    low = lax.ppermute(fields[:, ROWS - 1], "space", north)
    high = lax.ppermute(fields[:, 0], "space", [(j, i) for i, j in north])
    packed = jax.ShapeDtypeStruct((PACK, PACK), BF16)
    sent = call(
        forecast_kernel,
        packed,
        fields,
        low,
        high,
        conv_weight,
        norm_gain.reshape(CHANNELS, 1),
        weight_in,
        weight_out,
        scratch_shapes=[pltpu.VMEM((ROWS, 2, CHANNELS, WIDE), F32)],
    )

    def exchange(block):
        block = block.reshape(TILES, 2 * SUB, PACK)
        block = lax.all_to_all(block, "member", split_axis=0, concat_axis=0, tiled=True)
        return block.reshape(PACK, PACK)

    tile = exchange(sent)
    whole = pl.BlockSpec(memory_space=pltpu.VMEM)
    own = call(
        observe_kernel,
        jax.ShapeDtypeStruct((MEMBERS, 128), F32),
        obs_count,
        tile,
        obs_point[0],
        obs_channel[0],
        obs_value[0],
        obs_precision[0],
        in_specs=[pl.BlockSpec(memory_space=pltpu.SMEM)] + [whole] * 5,
    )
    around = lax.axis_size("member")
    ahead = [(i, (i + 1) % around) for i in range(around)]
    before = lax.ppermute(own, "member", ahead)
    after = lax.ppermute(own, "member", [(j, i) for i, j in ahead])
    returned = exchange(call(blend_kernel, packed, own, before, after, tile))
    result = call(unpack_kernel, jax.ShapeDtypeStruct((2, ROWS, CHANNELS, LON), BF16), returned)
    return result.transpose(0, 2, 1, 3)


def solution(mesh):
    in_specs = (
        P("member", None, "space", None),
        P(),
        P(),
        P(),
        P(),
        P("space", "member"),
        P("space", "member", None),
        P("space", "member", None),
        P("space", "member", None),
        P("space", "member", None),
    )
    out_specs = P("member", None, "space", None)
    return jax.shard_map(body, mesh=mesh, in_specs=in_specs, out_specs=out_specs, check_vma=False)
```

time: 133 us -> 79.7 us (0.60)
  the two profiles are of different devices: /device:TPU:2 before, /device:TPU:34 now
where the time goes in v1:
time: 79.7 us; the launch traced here: 79.3 us
  blocking collectives  26.1 us (33%)
  waiting for transfers between devices  21 us (26%)
  starting transfers between devices  19.3 us (24%)
  Pallas kernels  8.4 us (11%)
  local copies, waits for them, and re-layouts  3.77 us (5%)
    all_to_all x1, blocking collectives, exchange(): lax.all_to_all(block, 'member', split_axis=0, concat_axis=0, tiled=True)  26.1 us
    all_to_all x1, waiting for transfers between devices, exchange(): lax.all_to_all(block, 'member', split_axis=0, concat_axis=0, tiled=True)  17.6 us
    all_to_all x1, starting transfers between devices, exchange(): lax.all_to_all(block, 'member', split_axis=0, concat_axis=0, tiled=True)  11.5 us
    pallas_call x4, Pallas kernels, call(): pl.pallas_call(kernel, out_shape=out_shape, compiler_params=pltpu.Compile...  8.4 us
    ppermute x1, starting transfers between devices, body(): high = lax.ppermute(fields[:, 0], 'space', [(j, i) for i, j in north])  3.77 us
    unnamed x19, local copies, waits for them, and re-layouts  2.62 us
    ppermute x1, starting transfers between devices, body(): after = lax.ppermute(own, 'member', [(j, i) for i, j in ahead])  2.01 us
    ppermute x1, starting transfers between devices, body(): low = lax.ppermute(fields[:, ROWS - 1], 'space', north)  1.92 us
  transfers between devices with their start and end apart: 5, of which 4 were waited for; matrix products, arithmetic and copies ran while one was open for 0% of the time, Pallas kernels for 0%

profile of v1, /device:TPU:34, one launch (start us, length us, event | category | flops | bytes accessed | tf_op | source)
XLA Modules:
  0.0 79.3 jit_solution(16210307995477135851)
XLA Ops:
  0.0 1.1 %copy.18 = bf16[2,80,4,360]{3,1,0,2:T(8,128)(2,1)S(1)} copy(bf16[2,80,4,360]{3,2,1,0:T(4,128)(2,1)} %param.10) | data formatting | bytes 921600 | tf_op args[0]
  1.1 1.9 %collective-permute-start = (bf16[2,80,384]{2,1,0:T(8,128)(2,1)S(1)}, bf16[2,80,384]{2,1,0:T(8,128)(2,1)S(1)}, u32[]{:S(2)}, u32[]{:S(2)}) collective-permute-start(bf16[2,80,384]{2,1,0:T(8,128)(2,1)S(1)} %get-tuple-element.6), channel_id=1, source_target_pairs={{0,1},{1,2},{2,3},{3,4},{4,5},{5,6},{6,7},{8,9},{9,10},{10,11},{11... | collective-permute-start | bytes 368648 | tf_op jit(solution)/shard_map/ppermute | solution.py:237
  3.1 0.0 copy-start.6
  3.1 3.8 %collective-permute-start.1 = (bf16[2,80,384]{2,1,0:T(8,128)(2,1)S(1)}, bf16[2,80,384]{2,1,0:T(8,128)(2,1)S(1)}, u32[]{:S(2)}, u32[]{:S(2)}) collective-permute-start(bf16[2,80,384]{2,1,0:T(8,128)(2,1)S(1)} %get-tuple-element.5), channel_id=1, source_target_pairs={{1,0},{2,1},{3,2},{4,3},{5,4},{6,5},{7,6},{9,8},{10,9},{11,10},{12... | collective-permute-start | bytes 368648 | tf_op jit(solution)/shard_map/ppermute | solution.py:238
  6.9 0.1 copy.17
  6.9 0.1 copy.14.first_ref
  7.0 0.0 copy-start.7
  7.1 0.7 copy-done.7
  7.7 0.1 copy.13.gain_ref
  7.8 0.1 pad.4.clone.x_ref
  7.9 1.4 %collective-permute-done.1.high_ref = bf16[2,80,384]{2,1,0:T(8,128)(2,1)S(1)} collective-permute-done((bf16[2,80,384]{2,1,0:T(8,128)(2,1)S(1)}, bf16[2,80,384]{2,1,0:T(8,128)(2,1)S(1)}, u32[]{:S(2)}, u32[]{:S(2)}) %collective-permute-start.1) | collective-permute-done | bytes 122912 | tf_op jit(solution)/shard_map/ppermute | solution.py:238
  9.3 4.5 %shard_map.100 = bf16[512,512]{1,0:T(8,128)(2,1)} custom-call(bf16[2,4,80,384]{3,2,1,0:T(8,128)(2,1)S(1)} %pad.4.clone.x_ref, bf16[2,80,384]{2,1,0:T(8,128)(2,1)S(1)} %collective-permute-done.low_ref, bf16[2,80,384]{2,1,0:T(8,128)(2,1)S(1)} %collective-permute-done.1.high_ref, bf16[1,9,80,80]{3,2,1,0:T(8,128)(2,1)S(1)} %copy-done, ...), custom_call_target="tpu_custom_call" | custom-call | tf_op jit(solution)/shard_map/pallas_call | solution.py:214
  13.8 11.5 %all-to-all-start = ((bf16[32,16,512]{2,1,0:T(8,128)(2,1)}), bf16[32,16,512]{2,1,0:T(8,128)(2,1)S(1)}, u32[]{:S(2)}, u32[]{:S(2)}) async-start(bf16[32,16,512]{2,1,0:T(8,128)(2,1)} %bitcast.4), calls=%async_computation | async-start | bytes 1048576 | tf_op jit(solution)/shard_map/all_to_all | solution.py:255
  25.9 17.6 %all-to-all-done = bf16[32,16,512]{2,1,0:T(8,128)(2,1)S(1)} async-done(((bf16[32,16,512]{2,1,0:T(8,128)(2,1)}), bf16[32,16,512]{2,1,0:T(8,128)(2,1)S(1)}, u32[]{:S(2)}, u32[]{:S(2)}) %all-to-all-start) | async-done | bytes 524320 | tf_op jit(solution)/shard_map/all_to_all | solution.py:255
  43.6 0.7 copy-done.2
  44.2 0.6 shard_map.101.own_ref
  44.8 0.1 collective-permute-start.2
  44.9 2.0 %collective-permute-start.3 = (f32[64,128]{1,0:T(8,128)S(1)}, f32[64,128]{1,0:T(8,128)S(1)}, u32[]{:S(2)}, u32[]{:S(2)}) collective-permute-start(f32[64,128]{1,0:T(8,128)S(1)} %shard_map.101.own_ref), channel_id=1, source_target_pairs={{8,0},{16,8},{24,16},{32,24},{40,32},{48,40},{56,48},{64,56},{72,6... | collective-permute-start | bytes 98312 | tf_op jit(solution)/shard_map/ppermute | solution.py:274
  46.9 1.9 %collective-permute-done.2.before_ref = f32[64,128]{1,0:T(8,128)S(1)} collective-permute-done((f32[64,128]{1,0:T(8,128)S(1)}, f32[64,128]{1,0:T(8,128)S(1)}, u32[]{:S(2)}, u32[]{:S(2)}) %collective-permute-start.2) | collective-permute-done | bytes 32800 | tf_op jit(solution)/shard_map/ppermute | solution.py:273
  48.8 0.1 collective-permute-done.3.after_ref
  48.9 2.7 %shard_map.102 = bf16[512,512]{1,0:T(8,128)(2,1)S(1)} custom-call(f32[64,128]{1,0:T(8,128)S(1)} %shard_map.101.own_ref, f32[64,128]{1,0:T(8,128)S(1)} %collective-permute-done.2.before_ref, f32[64,128]{1,0:T(8,128)S(1)} %collective-permute-done.3.after_ref, bf16[512,512]{1,0:T(8,128)(2,1)S(1)} %bitcast.18), custom_call_target="tpu_custom_call" | custom-call | tf_op jit(solution)/shard_map/pallas_call | solution.py:214
  51.6 26.1 %all_to_all.10 = bf16[32,16,512]{2,1,0:T(8,128)(2,1)S(1)} all-to-all(bf16[32,16,512]{2,1,0:T(8,128)(2,1)S(1)} %bitcast.19), channel_id=1, replica_groups=mesh['member'=32,'space'=8] {'member'}, dimensions={0} | all-to-all | bytes 1048576 | tf_op jit(solution)/shard_map/all_to_all | solution.py:255
  77.7 0.7 shard_map.103
  78.4 1.0 %copy.15 = bf16[2,80,4,360]{3,2,1,0:T(4,128)(2,1)} copy(bf16[2,80,4,360]{3,1,2,0:T(8,128)(2,1)S(1)} %bitcast.21) | data formatting | bytes 921600 | tf_op jit(solution)/shard_map/transpose | solution.py:277
  (14 shorter events, 0.1 us)
Async XLA Ops:
  1.1 6.8 %collective-permute-start = (bf16[2,80,384]{2,1,0:T(8,128)(2,1)S(1)}, bf16[2,80,384]{2,1,0:T(8,128)(2,1)S(1)}, u32[]{:S(2)}, u32[]{:S(2)}) collective-permute-start(bf16[2,80,384]{2,1,0:T(8,128)(2,1)S(1)} %get-tuple-element.6), channel_id=1, source_target_pairs={{0,1},{1,2},{2,3},{3,4},{4,5},{5,6},{6,7},{8,9},{9,10},{10,11},{11... | collective-permute-start | bytes 368648 | tf_op jit(solution)/shard_map/ppermute | solution.py:237
  3.1 3.9 %copy-start.6 = (bf16[1,320,80]{1,2,0:T(8,128)(2,1)S(1)}, bf16[1,320,80]{1,2,0:T(8,128)(2,1)}, u32[]{:S(2)}) copy-start(bf16[1,320,80]{1,2,0:T(8,128)(2,1)} %param.13) | copy-start | bytes 153604
  3.1 6.2 %collective-permute-start.1 = (bf16[2,80,384]{2,1,0:T(8,128)(2,1)S(1)}, bf16[2,80,384]{2,1,0:T(8,128)(2,1)S(1)}, u32[]{:S(2)}, u32[]{:S(2)}) collective-permute-start(bf16[2,80,384]{2,1,0:T(8,128)(2,1)S(1)} %get-tuple-element.5), channel_id=1, source_target_pairs={{1,0},{2,1},{3,2},{4,3},{5,4},{6,5},{7,6},{9,8},{10,9},{11,10},{12... | collective-permute-start | bytes 368648 | tf_op jit(solution)/shard_map/ppermute | solution.py:238
  7.0 0.7 copy-start.7
  7.8 1.5 %copy-start = (bf16[1,9,80,80]{3,2,1,0:T(8,128)(2,1)S(1)}, bf16[1,9,80,80]{3,2,1,0:T(8,128)(2,1)}, u32[]{:S(2)}) copy-start(bf16[1,9,80,80]{3,2,1,0:T(8,128)(2,1)} %conv_ref.1) | copy-start | bytes 345604
  7.8 1.5 %copy-start.1 = (bf16[1,80,320]{2,1,0:T(8,128)(2,1)S(1)}, bf16[1,80,320]{2,1,0:T(8,128)(2,1)}, u32[]{:S(2)}) copy-start(bf16[1,80,320]{2,1,0:T(8,128)(2,1)} %second_ref.1) | copy-start | bytes 153604
  13.8 29.8 %copy-start.3 = (s32[1,1,256]{2,1,0:T(1,128)S(1)}, s32[1,1,256]{2,1,0:T(1,128)}, u32[]{:S(2)}) copy-start(s32[1,1,256]{2,1,0:T(1,128)} %param.17) | copy-start | bytes 3076
  13.8 29.8 %copy-start.4 = (f32[1,1,256]{2,1,0:T(1,128)S(1)}, f32[1,1,256]{2,1,0:T(1,128)}, u32[]{:S(2)}) copy-start(f32[1,1,256]{2,1,0:T(1,128)} %param.18) | copy-start | bytes 3076
  13.8 29.8 %copy-start.5 = (f32[1,1,256]{2,1,0:T(1,128)S(1)}, f32[1,1,256]{2,1,0:T(1,128)}, u32[]{:S(2)}) copy-start(f32[1,1,256]{2,1,0:T(1,128)} %param.19) | copy-start | bytes 3076
  13.8 29.8 %all-to-all-start = ((bf16[32,16,512]{2,1,0:T(8,128)(2,1)}), bf16[32,16,512]{2,1,0:T(8,128)(2,1)S(1)}, u32[]{:S(2)}, u32[]{:S(2)}) async-start(bf16[32,16,512]{2,1,0:T(8,128)(2,1)} %bitcast.4), calls=%async_computation | async-start | bytes 1048576 | tf_op jit(solution)/shard_map/all_to_all | solution.py:255
  43.5 0.7 copy-start.2
  44.8 4.0 %collective-permute-start.2 = (f32[64,128]{1,0:T(8,128)S(1)}, f32[64,128]{1,0:T(8,128)S(1)}, u32[]{:S(2)}, u32[]{:S(2)}) collective-permute-start(f32[64,128]{1,0:T(8,128)S(1)} %shard_map.101.own_ref), channel_id=1, source_target_pairs={{0,8},{8,16},{16,24},{24,32},{32,40},{40,48},{48,56},{56,64},{64,7... | collective-permute-start | bytes 98312 | tf_op jit(solution)/shard_map/ppermute | solution.py:273
  44.9 4.0 %collective-permute-start.3 = (f32[64,128]{1,0:T(8,128)S(1)}, f32[64,128]{1,0:T(8,128)S(1)}, u32[]{:S(2)}, u32[]{:S(2)}) collective-permute-start(f32[64,128]{1,0:T(8,128)S(1)} %shard_map.101.own_ref), channel_id=1, source_target_pairs={{8,0},{16,8},{24,16},{32,24},{40,32},{48,40},{56,48},{64,56},{72,6... | collective-permute-start | bytes 98312 | tf_op jit(solution)/shard_map/ppermute | solution.py:274

commit v2 on v1

v2 whole, which is shorter than its diff:
```python
import jax
import jax.numpy as jnp
from jax import lax
from jax.experimental import pallas as pl
from jax.experimental.pallas import tpu as pltpu
from jax.sharding import PartitionSpec as P

NS_STEPS = 6
NEAR_WEIGHT = 0.5
EPSILON = 1e-06
MEMBERS = 64
CHANNELS = 80
ROWS = 4
LON = 360
WIDE = 384
POINTS = 45
TILES = 32
PER_ROW = 8
SUB = 8
SLOTS = CHANNELS // SUB
PACK = 512
OBS = 256
HID = 320

F32 = jnp.float32
BF16 = jnp.bfloat16


def mm(left, right):
    return jnp.dot(left, right, preferred_element_type=F32)


def mm_t(left, right):
    return lax.dot_general(left, right, (((1,), (1,)), ((), ())), preferred_element_type=F32)


def halves(value):
    high = value.astype(BF16)
    return high, (value - high.astype(F32)).astype(BF16)


def mm_split(left, right, product=mm):
    left_high, left_low = halves(left)
    right_high, right_low = halves(right)
    return product(left_high, right_high) + (
        product(left_high, right_low) + product(left_low, right_high)
    )


def pieces(source, target, length):
    found = []
    done = 0
    while done < length:
        a, b = source + done, target + done
        step = min(length - done, 128 - a % 128, 128 - b % 128)
        found.append((a // 128, b // 128, (b - a) % 128, b % 128, b % 128 + step))
        done += step
    return found


def move(value, shift):
    return pltpu.roll(value, shift, 1) if shift else value


def shift_wrapped(west, here, east, lane):
    end = (LON - 1) % 128
    west_wrap = move(west[:, 256:], 128 - end)
    east_wrap = move(east[:, :128], end)
    west = pltpu.roll(west, 1, 1)
    east = pltpu.roll(east, WIDE - 1, 1)
    west = jnp.concatenate([jnp.where(lane == 0, west_wrap, west[:, :128]), west[:, 128:]], axis=1)
    east = jnp.concatenate([east[:, :256], jnp.where(lane == end, east_wrap, east[:, 256:])], axis=1)
    return here + west + east


def forecast_rows(windows, conv_ref, gain_ref, first_ref, second_ref, held):
    conv = conv_ref[...]
    first = first_ref[...]
    second = second_ref[...]
    gain = gain_ref[:, :1]
    lane = lax.broadcasted_iota(jnp.int32, (CHANNELS, 128), 1)
    for m in range(2):
        near, far = windows[m]
        stacked = jnp.concatenate(
            [jnp.concatenate([near[a], far[a]], axis=1) for a in range(3)], axis=0
        )
        taps = mm(conv, stacked)
        parts = []
        for d, window in enumerate(windows[m]):
            west, here, east = [
                taps[CHANNELS * b : CHANNELS * (b + 1), WIDE * d : WIDE * (d + 1)] for b in range(3)
            ]
            parts.append(window[1].astype(F32) + shift_wrapped(west, here, east, lane))
        updated = jnp.concatenate(parts, axis=1)
        power = jnp.sum(updated * updated, axis=0, keepdims=True) * (1.0 / CHANNELS)
        normed = (updated * lax.rsqrt(power + EPSILON) * gain).astype(BF16)
        hidden = mm(first, normed)
        hidden = (hidden * (0.5 + 0.5 * jnp.tanh(0.5 * hidden))).astype(BF16)
        result = updated + mm(second, hidden)
        held[0, m] = result[:, :WIDE]
        held[1, m] = result[:, WIDE:]


def pack_rows(held, starts, out_ref):
    spot = lax.broadcasted_iota(jnp.int32, (2 * SUB, 128), 1)
    for i, start in enumerate(starts):
        for j in range(PER_ROW):
            packed = [jnp.zeros((2 * SUB, 128), F32) for _ in range(PACK // 128)]
            for s in range(SLOTS):
                for a, b, shift, low, high in pieces(j * POINTS, s * POINTS, POINTS):
                    both = held[i, :, s * SUB : (s + 1) * SUB, a * 128 : (a + 1) * 128]
                    both = move(both.reshape(2 * SUB, 128), shift)
                    packed[b] = jnp.where((spot >= low) & (spot < high), both, packed[b])
            at = start + j * 2 * SUB
            out_ref[at : at + 2 * SUB, :] = jnp.concatenate(packed, axis=1).astype(BF16)


ROW_PACK = PER_ROW * 2 * SUB


def inner_kernel(
    x_ref,
    conv,
    gain,
    first,
    count,
    point,
    channel,
    value,
    precision,
    second_ref,
    out_ref,
    conv_ref,
    gain_ref,
    first_ref,
    obs_ref,
    held,
):
    conv_ref[...] = jnp.concatenate(
        [conv[0, 3 * a : 3 * a + 3].reshape(3 * CHANNELS, CHANNELS) for a in range(3)], axis=1
    )
    row = lax.broadcasted_iota(jnp.int32, (CHANNELS, CHANNELS), 0)
    column = lax.broadcasted_iota(jnp.int32, (CHANNELS, CHANNELS), 1)
    tall = jnp.sum(jnp.where(row == column, gain[...], 0.0), axis=1, keepdims=True)
    gain_ref[...] = jnp.broadcast_to(tall, (CHANNELS, 128))
    first_ref[...] = first[...].astype(F32).T.astype(BF16)
    slots = lax.broadcasted_iota(jnp.int32, (1, OBS), 1)
    obs_ref[0:1, :] = ((channel[...] // SUB) * POINTS + point[...]).astype(F32)
    obs_ref[1:2, :] = (channel[...] % SUB).astype(F32)
    obs_ref[2:3, :] = jnp.where(slots < count[...], precision[...], 0.0)
    obs_ref[3:4, :] = value[...]
    obs_ref[4:, :] = jnp.zeros((4, OBS), F32)
    windows = [[[x_ref[m, r + d] for d in (-1, 0, 1)] for r in (1, 2)] for m in range(2)]
    forecast_rows(windows, conv_ref, gain_ref, first_ref, second_ref, held)
    pack_rows(held, (0, ROW_PACK), out_ref)


def outer_kernel(
    odd_ref,
    x_ref,
    chip_ref,
    next_ref,
    inner_ref,
    conv_ref,
    gain_ref,
    first_ref,
    second_ref,
    out_ref,
    held,
):
    odd = odd_ref[...] == 1
    windows = []
    for m in range(2):
        low = jnp.where(odd, chip_ref[m].astype(F32), next_ref[m].astype(F32)).astype(BF16)
        high = jnp.where(odd, next_ref[m].astype(F32), chip_ref[m].astype(F32)).astype(BF16)
        windows.append([[low, x_ref[m, 0], x_ref[m, 1]], [x_ref[m, 2], x_ref[m, 3], high]])
    forecast_rows(windows, conv_ref, gain_ref, first_ref, second_ref, held)
    pack_rows(held, (0, 3 * ROW_PACK), out_ref)
    out_ref[ROW_PACK : 3 * ROW_PACK, :] = inner_ref[...]


def observe_kernel(tile_ref, obs_ref, out_ref):
    place = lax.broadcasted_iota(jnp.int32, (PACK, OBS), 0)
    lane = obs_ref[0:1, :].astype(jnp.int32)
    sub = obs_ref[1:2, :].astype(jnp.int32)
    weight = obs_ref[2:3, :]
    found = mm(tile_ref[...], jnp.where(place == lane, 1.0, 0.0).astype(BF16))
    found = jnp.where(place % SUB == sub, found, 0.0)
    sampled = jnp.sum(found.reshape(MEMBERS, SUB, OBS), axis=1)
    average = jnp.sum(sampled, axis=0, keepdims=True) * (1.0 / MEMBERS)
    spread = sampled - average
    innovation = obs_ref[3:4, :] - average
    gram = mm_split(spread * weight, spread, mm_t)
    out_ref[: MEMBERS // 2, :MEMBERS] = gram[: MEMBERS // 2]
    out_ref[: MEMBERS // 2, MEMBERS:] = gram[MEMBERS // 2 :]
    pull = jnp.broadcast_to(weight * innovation, (8, OBS))
    out_ref[MEMBERS // 2 :, :MEMBERS] = mm_split(pull, spread, mm_t)
    out_ref[MEMBERS // 2 :, MEMBERS:] = jnp.zeros((8, MEMBERS), F32)


def blend_kernel(own_ref, far_ref, near_ref, tile_ref, out_ref):
    total = own_ref[...] + NEAR_WEIGHT * (far_ref[...] + near_ref[...])
    gram = jnp.concatenate([total[: MEMBERS // 2, :MEMBERS], total[: MEMBERS // 2, MEMBERS:]], axis=0)
    vector = total[MEMBERS // 2 : MEMBERS // 2 + 1, :MEMBERS]
    identity = jnp.where(
        lax.broadcasted_iota(jnp.int32, (MEMBERS, MEMBERS), 0)
        == lax.broadcasted_iota(jnp.int32, (MEMBERS, MEMBERS), 1),
        1.0,
        0.0,
    )
    system = (MEMBERS - 1.0) * identity + gram
    squares = jnp.sum(jnp.sum(system * system, axis=0, keepdims=True), axis=1, keepdims=True)
    scale = jnp.sqrt(squares)
    root = system / scale
    middle = 1.5 * identity - 0.5 * root
    root = mm_split(root, middle)
    inverse = middle
    for sweep in range(1, NS_STEPS):
        middle = 1.5 * identity - 0.5 * mm_split(inverse, root)
        if sweep < NS_STEPS - 1:
            root = mm_split(root, middle)
        inverse = mm_split(middle, inverse)
    once = jnp.sum(inverse * vector, axis=1, keepdims=True)
    mean_weight = jnp.sum(inverse * once, axis=0, keepdims=True) / scale
    full = jnp.sqrt((MEMBERS - 1.0) / scale) * inverse + mean_weight
    mixing = full + (1.0 - jnp.sum(full, axis=1, keepdims=True)) * (1.0 / MEMBERS)
    mixing = mixing.astype(BF16)
    spread_cols = jnp.where(
        lax.broadcasted_iota(jnp.int32, (MEMBERS, PACK), 1) // SUB
        == lax.broadcasted_iota(jnp.int32, (MEMBERS, PACK), 0),
        1.0,
        0.0,
    ).astype(BF16)
    wide = mm(mixing, spread_cols)
    square = jnp.broadcast_to(wide[:, None, :], (MEMBERS, SUB, PACK)).reshape(PACK, PACK)
    same = (
        lax.broadcasted_iota(jnp.int32, (PACK, PACK), 0) % SUB
        == lax.broadcasted_iota(jnp.int32, (PACK, PACK), 1) % SUB
    )
    square = jnp.where(same, square, 0.0).astype(BF16)
    out_ref[...] = mm(square, tile_ref[...]).astype(BF16)


def unpack_kernel(in_ref, out_ref):
    spot = lax.broadcasted_iota(jnp.int32, (2 * SUB, 128), 1)

    @pl.loop(0, ROWS)
    def _(r):
        for pair in range(SLOTS // 2):
            lines = []
            for s in (2 * pair, 2 * pair + 1):
                line = [jnp.zeros((2 * SUB, 128), F32) for _ in range(WIDE // 128)]
                for j in range(PER_ROW):
                    at = pl.multiple_of((r * PER_ROW + j) * 2 * SUB, 2 * SUB)
                    for a, b, shift, start, stop in pieces(s * POINTS, j * POINTS, POINTS):
                        both = in_ref[pl.ds(at, 2 * SUB), a * 128 : (a + 1) * 128].astype(F32)
                        line[b] = jnp.where((spot >= start) & (spot < stop), move(both, shift), line[b])
                lines.append(jnp.concatenate(line, axis=1))
            for m in range(2):
                joined = jnp.concatenate([line[m * SUB : (m + 1) * SUB] for line in lines], axis=0)
                out_ref[m, r, pair * 2 * SUB : (pair + 1) * 2 * SUB, :] = joined.astype(BF16)[:, :LON]


def call(kernel, out_shape, *operands, **more):
    return pl.pallas_call(
        kernel,
        out_shape=out_shape,
        compiler_params=pltpu.CompilerParams(vmem_limit_bytes=40 * 1024 * 1024),
        **more,
    )(*operands)


def body(
    starting_fields,
    conv_weight,
    norm_gain,
    weight_in,
    weight_out,
    obs_count,
    obs_point,
    obs_channel,
    obs_value,
    obs_precision,
):
    fields = jnp.pad(starting_fields.transpose(0, 2, 1, 3), ((0, 0), (0, 0), (0, 0), (0, WIDE - LON)))
    fields = lax.optimization_barrier(fields)
    bands = lax.axis_size("space")
    odd = lax.axis_index("space") % 2
    top, bottom = fields[:, 0], fields[:, ROWS - 1]
    across = [(i, i + 1 if i % 2 else i - 1) for i in range(1, bands - 1)]
    next_row = lax.ppermute(jnp.where(odd == 1, bottom, top), "space", across)
    within = [(i, i ^ 1) for i in range(bands)]
    chip_row = lax.ppermute(jnp.where(odd == 1, top, bottom), "space", within)
    held = [pltpu.VMEM((2, 2, CHANNELS, WIDE), F32)]
    second = weight_out[0]
    inner, conv, gain, first, observations = call(
        inner_kernel,
        (
            jax.ShapeDtypeStruct((2 * ROW_PACK, PACK), BF16),
            jax.ShapeDtypeStruct((3 * CHANNELS, 3 * CHANNELS), BF16),
            jax.ShapeDtypeStruct((CHANNELS, 128), F32),
            jax.ShapeDtypeStruct((HID, CHANNELS), BF16),
            jax.ShapeDtypeStruct((8, OBS), F32),
        ),
        fields,
        conv_weight,
        norm_gain,
        weight_in[0].T,
        obs_count,
        obs_point[0],
        obs_channel[0],
        obs_value[0],
        obs_precision[0],
        second,
        scratch_shapes=held,
        cost_estimate=pl.CostEstimate(flops=400_000_000, bytes_accessed=2_000_000, transcendentals=500_000),
    )
    weights = (conv, gain, first, second)
    packed = jax.ShapeDtypeStruct((PACK, PACK), BF16)
    sent = call(
        outer_kernel, packed, odd.reshape(1, 1), fields, chip_row, next_row, inner, *weights, scratch_shapes=held
    )

    def exchange(block):
        block = block.reshape(TILES, 2 * SUB, PACK)
        block = lax.all_to_all(block, "member", split_axis=0, concat_axis=0, tiled=True)
        return block.reshape(PACK, PACK)

    tile = exchange(sent)
    own = call(observe_kernel, jax.ShapeDtypeStruct((MEMBERS // 2 + 8, 128), F32), tile, observations)
    around = lax.axis_size("member")
    far = lax.ppermute(own, "member", [(i, (i + 1 if i % 2 else i - 1) % around) for i in range(around)])
    near = lax.ppermute(own, "member", [(i, i ^ 1) for i in range(around)])
    returned = exchange(call(blend_kernel, packed, own, far, near, tile))
    result = call(unpack_kernel, jax.ShapeDtypeStruct((2, ROWS, CHANNELS, LON), BF16), returned)
    return result.transpose(0, 2, 1, 3)


def solution(mesh):
    in_specs = (
        P("member", None, "space", None),
        P(),
        P(),
        P(),
        P(),
        P("space", "member"),
        P("space", "member", None),
        P("space", "member", None),
        P("space", "member", None),
        P("space", "member", None),
    )
    out_specs = P("member", None, "space", None)
    return jax.shard_map(body, mesh=mesh, in_specs=in_specs, out_specs=out_specs, check_vma=False)
```

time: 79.7 us -> 70.9 us (0.89)
  the two profiles are of different devices: /device:TPU:34 before, /device:TPU:38 now
where the time goes in v2:
time: 70.9 us; the launch traced here: 69.8 us
  blocking collectives  51.8 us (73%)
  Pallas kernels  7.55 us (11%)
  starting transfers between devices  4.04 us (6%)
  local copies, waits for them, and re-layouts  2.87 us (4%)
  waiting for transfers between devices  2.72 us (4%)
  between operations  0.81 us (1%)
    all_to_all x2, blocking collectives, exchange(): lax.all_to_all(block, 'member', split_axis=0, concat_axis=0, tiled=True)  51.8 us
    pallas_call x5, Pallas kernels, call(): pl.pallas_call(kernel, out_shape=out_shape, compiler_params=pltpu.Compile...  7.55 us
    ppermute x1, starting transfers between devices, body(): next_row = lax.ppermute(jnp.where(odd == 1, bottom, top), 'space', across)  2.18 us
    ppermute x1, waiting for transfers between devices, body(): near = lax.ppermute(own, 'member', [(i, i ^ 1) for i in range(around)])  2.07 us
    unnamed x17, local copies, waits for them, and re-layouts  1.8 us
    ppermute x1, starting transfers between devices, body(): lax.ppermute(own, 'member', [(i, (i + 1 if i % 2 else i - 1) % around) fo...  1.7 us
  transfers between devices with their start and end apart: 4, of which 3 were waited for; matrix products, arithmetic and copies ran while one was open for 0% of the time, Pallas kernels for 3%

profile of v2, /device:TPU:38, one launch (start us, length us, event | category | flops | bytes accessed | tf_op | source)
XLA Modules:
  0.0 69.8 jit_solution(12080693750068679367)
XLA Ops:
  0.0 1.1 %copy.16 = bf16[2,80,4,360]{3,1,0,2:T(8,128)(2,1)S(1)} copy(bf16[2,80,4,360]{3,2,1,0:T(4,128)(2,1)} %param.10) | data formatting | bytes 921600 | tf_op args[0]
  1.1 0.1 pad.4
  1.2 2.2 %collective-permute-start.1 = (bf16[2,80,384]{2,1,0:T(8,128)(2,1)S(1)}, bf16[2,80,384]{2,1,0:T(8,128)(2,1)S(1)}, u32[]{:S(2)}, u32[]{:S(2)}) collective-permute-start(bf16[2,80,384]{2,1,0:T(8,128)(2,1)S(1)} %get-tuple-element.15), channel_id=1, source_target_pairs={{1,2},{2,1},{3,4},{4,3},{5,6},{6,5},{9,10},{10,9},{11,12},{12,11},... | collective-permute-start | bytes 368648 | tf_op jit(solution)/shard_map/ppermute | solution.py:291
  3.4 0.0 copy-start
  3.4 0.0 copy-start.1
  3.4 0.0 copy-start.2
  3.4 0.1 collective-permute-start
  3.5 0.0 copy-start.4
  3.6 0.1 copy.13.x_ref
  4.3 0.0 copy-done.1
  4.4 0.6 copy-done.3
  5.0 1.9 %shard_map.100 = (bf16[256,512]{1,0:T(8,128)(2,1)S(1)}, bf16[240,240]{1,0:T(8,128)(2,1)S(1)}, f32[80,128]{1,0:T(8,128)S(1)}, bf16[320,80]{1,0:T(8,128)(2,1)S(1)}, f32[8,256]{1,0:T(8,128)S(1)}) custom-call(bf16[2,4,80,384]{3,2,1,0:T(8,128)(2,1)S(1)} %copy.13.x_ref, bf16[1,9,80,80]{3,2,1,0:T(8,128)(2,1)S(1)} %copy-done.1, f32[1,80]{1,0:T(1,128)S(1)} %copy-done.7, ...), custom_call_target="tpu_custom_call" | custom-call | flops 400000000 | bytes 2000000 | tf_op jit(solution)/shard_map/pallas_call | solution.py:265
  6.9 0.5 collective-permute-done.1.next_ref
  7.4 1.8 %shard_map.101 = bf16[512,512]{1,0:T(8,128)(2,1)S(1)} custom-call(s32[1,1]{1,0:T(1,128)} %bitcast.odd_ref, bf16[2,4,80,384]{3,2,1,0:T(8,128)(2,1)S(1)} %copy.13.x_ref, bf16[2,80,384]{2,1,0:T(8,128)(2,1)S(1)} %collective-permute-done.chip_ref, bf16[2,80,384]{2,1,0:T(8,128)(2,1)S(1)} %collective-permute-done.1.next_ref, ...), custom_call_target="tpu_custom_call" | custom-call | tf_op jit(solution)/shard_map/pallas_call | solution.py:265
  9.2 28.9 %all_to_all.10 = bf16[32,16,512]{2,1,0:T(8,128)(2,1)S(1)} all-to-all(bf16[32,16,512]{2,1,0:T(8,128)(2,1)S(1)} %bitcast.25), channel_id=1, replica_groups=mesh['member'=32,'space'=8] {'member'}, dimensions={0} | all-to-all | bytes 1048576 | tf_op jit(solution)/shard_map/all_to_all | solution.py:326
  38.1 0.6 shard_map.102.own_ref
  38.7 0.1 collective-permute-start.3
  38.8 1.7 %collective-permute-start.2 = (f32[40,128]{1,0:T(8,128)S(1)}, f32[40,128]{1,0:T(8,128)S(1)}, u32[]{:S(2)}, u32[]{:S(2)}) collective-permute-start(f32[40,128]{1,0:T(8,128)S(1)} %shard_map.102.own_ref), channel_id=1, source_target_pairs={{0,248},{8,16},{16,8},{24,32},{32,24},{40,48},{48,40},{56,64},{64,... | collective-permute-start | bytes 61448 | tf_op jit(solution)/shard_map/ppermute | solution.py:332
  40.5 2.1 %collective-permute-done.3.near_ref = f32[40,128]{1,0:T(8,128)S(1)} collective-permute-done((f32[40,128]{1,0:T(8,128)S(1)}, f32[40,128]{1,0:T(8,128)S(1)}, u32[]{:S(2)}, u32[]{:S(2)}) %collective-permute-start.3) | collective-permute-done | bytes 20512 | tf_op jit(solution)/shard_map/ppermute | solution.py:333
  42.6 0.1 collective-permute-done.2.far_ref
  42.7 2.5 %shard_map.103 = bf16[512,512]{1,0:T(8,128)(2,1)S(1)} custom-call(f32[40,128]{1,0:T(8,128)S(1)} %shard_map.102.own_ref, f32[40,128]{1,0:T(8,128)S(1)} %collective-permute-done.2.far_ref, f32[40,128]{1,0:T(8,128)S(1)} %collective-permute-done.3.near_ref, bf16[512,512]{1,0:T(8,128)(2,1)S(1)} %bitcast.22), custom_call_target="tpu_custom_call" | custom-call | tf_op jit(solution)/shard_map/pallas_call | solution.py:265
  45.2 22.9 %all_to_all.11 = bf16[32,16,512]{2,1,0:T(8,128)(2,1)S(1)} all-to-all(bf16[32,16,512]{2,1,0:T(8,128)(2,1)S(1)} %bitcast.23), channel_id=1, replica_groups=mesh['member'=32,'space'=8] {'member'}, dimensions={0} | all-to-all | bytes 1048576 | tf_op jit(solution)/shard_map/all_to_all | solution.py:326
  68.1 0.7 shard_map.104
  68.8 1.0 %copy.14 = bf16[2,80,4,360]{3,2,1,0:T(4,128)(2,1)} copy(bf16[2,80,4,360]{3,1,2,0:T(8,128)(2,1)S(1)} %bitcast.26) | data formatting | bytes 921600 | tf_op jit(solution)/shard_map/transpose | solution.py:336
  (12 shorter events, 0.1 us)
Async XLA Ops:
  1.2 6.2 %collective-permute-start.1 = (bf16[2,80,384]{2,1,0:T(8,128)(2,1)S(1)}, bf16[2,80,384]{2,1,0:T(8,128)(2,1)S(1)}, u32[]{:S(2)}, u32[]{:S(2)}) collective-permute-start(bf16[2,80,384]{2,1,0:T(8,128)(2,1)S(1)} %get-tuple-element.15), channel_id=1, source_target_pairs={{1,2},{2,1},{3,4},{4,3},{5,6},{6,5},{9,10},{10,9},{11,12},{12,11},... | collective-permute-start | bytes 368648 | tf_op jit(solution)/shard_map/ppermute | solution.py:291
  3.4 0.9 %copy-start = (bf16[1,80,320]{2,1,0:T(8,128)(2,1)S(1)}, bf16[1,80,320]{2,1,0:T(8,128)(2,1)}, u32[]{:S(2)}) copy-start(bf16[1,80,320]{2,1,0:T(8,128)(2,1)} %param.14) | copy-start | bytes 153604
  3.4 0.9 %copy-start.1 = (bf16[1,9,80,80]{3,2,1,0:T(8,128)(2,1)S(1)}, bf16[1,9,80,80]{3,2,1,0:T(8,128)(2,1)}, u32[]{:S(2)}) copy-start(bf16[1,9,80,80]{3,2,1,0:T(8,128)(2,1)} %conv.1) | copy-start | bytes 345604
  3.4 0.9 %copy-start.2 = (bf16[1,320,80]{1,2,0:T(8,128)(2,1)S(1)}, bf16[1,320,80]{1,2,0:T(8,128)(2,1)}, u32[]{:S(2)}) copy-start(bf16[1,320,80]{1,2,0:T(8,128)(2,1)} %param.13) | copy-start | bytes 153604
  3.4 4.0 %collective-permute-start = (bf16[2,80,384]{2,1,0:T(8,128)(2,1)S(1)}, bf16[2,80,384]{2,1,0:T(8,128)(2,1)S(1)}, u32[]{:S(2)}, u32[]{:S(2)}) collective-permute-start(bf16[2,80,384]{2,1,0:T(8,128)(2,1)S(1)} %get-tuple-element.16), channel_id=1, source_target_pairs={{0,1},{1,0},{2,3},{3,2},{4,5},{5,4},{6,7},{7,6},{8,9},{9,8},{10,11... | collective-permute-start | bytes 368648 | tf_op jit(solution)/shard_map/ppermute | solution.py:293
  3.5 0.8 %copy-start.4 = (s32[1,1,256]{2,1,0:T(1,128)S(1)}, s32[1,1,256]{2,1,0:T(1,128)}, u32[]{:S(2)}) copy-start(s32[1,1,256]{2,1,0:T(1,128)} %param.17) | copy-start | bytes 3076
  3.5 0.8 %copy-start.5 = (f32[1,1,256]{2,1,0:T(1,128)S(1)}, f32[1,1,256]{2,1,0:T(1,128)}, u32[]{:S(2)}) copy-start(f32[1,1,256]{2,1,0:T(1,128)} %param.18) | copy-start | bytes 3076
  3.5 0.8 %copy-start.6 = (f32[1,1,256]{2,1,0:T(1,128)S(1)}, f32[1,1,256]{2,1,0:T(1,128)}, u32[]{:S(2)}) copy-start(f32[1,1,256]{2,1,0:T(1,128)} %param.19) | copy-start | bytes 3076
  4.3 0.7 %copy-start.3 = (s32[1,1,256]{2,1,0:T(1,128)S(1)}, s32[1,1,256]{2,1,0:T(1,128)}, u32[]{:S(2)}) copy-start(s32[1,1,256]{2,1,0:T(1,128)} %param.16) | copy-start | bytes 3076
  4.3 0.7 %copy-start.7 = (f32[1,80]{1,0:T(1,128)S(1)}, f32[1,80]{1,0:T(1,128)}, u32[]{:S(2)}) copy-start(f32[1,80]{1,0:T(1,128)} %gain.1) | copy-start | bytes 964
  38.7 3.8 %collective-permute-start.3 = (f32[40,128]{1,0:T(8,128)S(1)}, f32[40,128]{1,0:T(8,128)S(1)}, u32[]{:S(2)}, u32[]{:S(2)}) collective-permute-start(f32[40,128]{1,0:T(8,128)S(1)} %shard_map.102.own_ref), channel_id=1, source_target_pairs={{0,8},{8,0},{16,24},{24,16},{32,40},{40,32},{48,56},{56,48},{64,72... | collective-permute-start | bytes 61448 | tf_op jit(solution)/shard_map/ppermute | solution.py:333
  38.8 3.9 %collective-permute-start.2 = (f32[40,128]{1,0:T(8,128)S(1)}, f32[40,128]{1,0:T(8,128)S(1)}, u32[]{:S(2)}, u32[]{:S(2)}) collective-permute-start(f32[40,128]{1,0:T(8,128)S(1)} %shard_map.102.own_ref), channel_id=1, source_target_pairs={{0,248},{8,16},{16,8},{24,32},{32,24},{40,48},{48,40},{56,64},{64,... | collective-permute-start | bytes 61448 | tf_op jit(solution)/shard_map/ppermute | solution.py:332

commit v3 on v2

--- a/solution.py
+++ b/solution.py
@@ -198,8 +198,8 @@
     out_ref[MEMBERS // 2 :, MEMBERS:] = jnp.zeros((8, MEMBERS), F32)
 
 
-def blend_kernel(own_ref, far_ref, near_ref, tile_ref, out_ref):
-    total = own_ref[...] + NEAR_WEIGHT * (far_ref[...] + near_ref[...])
+def blend_kernel(own_ref, near_ref, far_ref, tile_ref, out_ref):
+    total = own_ref[...] + NEAR_WEIGHT * (near_ref[...] + far_ref[...])
     gram = jnp.concatenate([total[: MEMBERS // 2, :MEMBERS], total[: MEMBERS // 2, MEMBERS:]], axis=0)
     vector = total[MEMBERS // 2 : MEMBERS // 2 + 1, :MEMBERS]
     identity = jnp.where(
@@ -331,7 +331,7 @@
     around = lax.axis_size("member")
     far = lax.ppermute(own, "member", [(i, (i + 1 if i % 2 else i - 1) % around) for i in range(around)])
     near = lax.ppermute(own, "member", [(i, i ^ 1) for i in range(around)])
-    returned = exchange(call(blend_kernel, packed, own, far, near, tile))
+    returned = exchange(call(blend_kernel, packed, own, near, far, tile))
     result = call(unpack_kernel, jax.ShapeDtypeStruct((2, ROWS, CHANNELS, LON), BF16), returned)
     return result.transpose(0, 2, 1, 3)
 

time: 70.9 us -> 70.2 us (level)
  blocking collectives: 51.8 us -> 50.6 us
    ppermute x1, starting transfers between devices: 0.07 us -> 1.86 us  [body(): near = lax.ppermute(own, 'member', [(i, i ^ 1) for i in range(around)])]
    ppermute x1, waiting for transfers between devices: 2.07 us -> 0.45 us  [body(): near = lax.ppermute(own, 'member', [(i, i ^ 1) for i in range(around)])]
    ppermute x1, waiting for transfers between devices: 0.1 us -> 1.47 us  [body(): lax.ppermute(own, 'member', [(i, (i + 1 if i % 2 else i - 1) % around) fo...]
    ppermute x1, starting transfers between devices: 1.7 us -> 0.51 us  [body(): lax.ppermute(own, 'member', [(i, (i + 1 if i % 2 else i - 1) % around) fo...]
    all_to_all x2, blocking collectives: 51.8 us -> 50.6 us  [exchange(): lax.all_to_all(block, 'member', split_axis=0, concat_axis=0, tiled=True)]
where the time goes in v3:
time: 70.2 us; the launch traced here: 69 us
  blocking collectives  50.6 us (72%)
  Pallas kernels  7.56 us (11%)
  starting transfers between devices  4.64 us (7%)
  local copies, waits for them, and re-layouts  2.87 us (4%)
  waiting for transfers between devices  2.47 us (4%)
  between operations  0.8 us (1%)
    all_to_all x2, blocking collectives, exchange(): lax.all_to_all(block, 'member', split_axis=0, concat_axis=0, tiled=True)  50.6 us
    pallas_call x5, Pallas kernels, call(): pl.pallas_call(kernel, out_shape=out_shape, compiler_params=pltpu.Compile...  7.56 us
    ppermute x1, starting transfers between devices, body(): next_row = lax.ppermute(jnp.where(odd == 1, bottom, top), 'space', across)  2.18 us
    ppermute x1, starting transfers between devices, body(): near = lax.ppermute(own, 'member', [(i, i ^ 1) for i in range(around)])  1.86 us
    unnamed x17, local copies, waits for them, and re-layouts  1.8 us
    ppermute x1, waiting for transfers between devices, body(): lax.ppermute(own, 'member', [(i, (i + 1 if i % 2 else i - 1) % around) fo...  1.47 us
  transfers between devices with their start and end apart: 4, of which 3 were waited for; matrix products, arithmetic and copies ran while one was open for 0% of the time, Pallas kernels for 3%

profile of v3, /device:TPU:38, one launch (start us, length us, event | category | flops | bytes accessed | tf_op | source)
XLA Modules:
  0.0 69.0 jit_solution(13842070503611100271)
XLA Ops:
  0.0 1.1 %copy.16 = bf16[2,80,4,360]{3,1,0,2:T(8,128)(2,1)S(1)} copy(bf16[2,80,4,360]{3,2,1,0:T(4,128)(2,1)} %param.10) | data formatting | bytes 921600 | tf_op args[0]
  1.1 0.1 pad.4
  1.2 2.2 %collective-permute-start.1 = (bf16[2,80,384]{2,1,0:T(8,128)(2,1)S(1)}, bf16[2,80,384]{2,1,0:T(8,128)(2,1)S(1)}, u32[]{:S(2)}, u32[]{:S(2)}) collective-permute-start(bf16[2,80,384]{2,1,0:T(8,128)(2,1)S(1)} %get-tuple-element.15), channel_id=1, source_target_pairs={{1,2},{2,1},{3,4},{4,3},{5,6},{6,5},{9,10},{10,9},{11,12},{12,11},... | collective-permute-start | bytes 368648 | tf_op jit(solution)/shard_map/ppermute | solution.py:291
  3.4 0.0 copy-start
  3.4 0.0 copy-start.1
  3.4 0.1 collective-permute-start
  3.5 0.0 copy-start.4
  3.5 0.0 copy-start.5
  3.6 0.1 copy.13.x_ref
  4.3 0.0 copy-done.1
  4.4 0.6 copy-done.3
  5.0 1.9 %shard_map.100 = (bf16[256,512]{1,0:T(8,128)(2,1)S(1)}, bf16[240,240]{1,0:T(8,128)(2,1)S(1)}, f32[80,128]{1,0:T(8,128)S(1)}, bf16[320,80]{1,0:T(8,128)(2,1)S(1)}, f32[8,256]{1,0:T(8,128)S(1)}) custom-call(bf16[2,4,80,384]{3,2,1,0:T(8,128)(2,1)S(1)} %copy.13.x_ref, bf16[1,9,80,80]{3,2,1,0:T(8,128)(2,1)S(1)} %copy-done.1, f32[1,80]{1,0:T(1,128)S(1)} %copy-done.7, ...), custom_call_target="tpu_custom_call" | custom-call | flops 400000000 | bytes 2000000 | tf_op jit(solution)/shard_map/pallas_call | solution.py:265
  6.9 0.5 collective-permute-done.1.next_ref
  7.4 1.8 %shard_map.101 = bf16[512,512]{1,0:T(8,128)(2,1)S(1)} custom-call(s32[1,1]{1,0:T(1,128)} %bitcast.odd_ref, bf16[2,4,80,384]{3,2,1,0:T(8,128)(2,1)S(1)} %copy.13.x_ref, bf16[2,80,384]{2,1,0:T(8,128)(2,1)S(1)} %collective-permute-done.chip_ref, bf16[2,80,384]{2,1,0:T(8,128)(2,1)S(1)} %collective-permute-done.1.next_ref, ...), custom_call_target="tpu_custom_call" | custom-call | tf_op jit(solution)/shard_map/pallas_call | solution.py:265
  9.2 28.9 %all_to_all.10 = bf16[32,16,512]{2,1,0:T(8,128)(2,1)S(1)} all-to-all(bf16[32,16,512]{2,1,0:T(8,128)(2,1)S(1)} %bitcast.25), channel_id=1, replica_groups=mesh['member'=32,'space'=8] {'member'}, dimensions={0} | all-to-all | bytes 1048576 | tf_op jit(solution)/shard_map/all_to_all | solution.py:326
  38.1 0.6 shard_map.102.own_ref
  38.7 0.5 collective-permute-start.3
  39.2 1.9 %collective-permute-start.2 = (f32[40,128]{1,0:T(8,128)S(1)}, f32[40,128]{1,0:T(8,128)S(1)}, u32[]{:S(2)}, u32[]{:S(2)}) collective-permute-start(f32[40,128]{1,0:T(8,128)S(1)} %shard_map.102.own_ref), channel_id=1, source_target_pairs={{0,8},{8,0},{16,24},{24,16},{32,40},{40,32},{48,56},{56,48},{64,72... | collective-permute-start | bytes 61448 | tf_op jit(solution)/shard_map/ppermute | solution.py:333
  41.1 1.5 %collective-permute-done.3.far_ref = f32[40,128]{1,0:T(8,128)S(1)} collective-permute-done((f32[40,128]{1,0:T(8,128)S(1)}, f32[40,128]{1,0:T(8,128)S(1)}, u32[]{:S(2)}, u32[]{:S(2)}) %collective-permute-start.3) | collective-permute-done | bytes 20512 | tf_op jit(solution)/shard_map/ppermute | solution.py:332
  42.6 0.4 collective-permute-done.2.near_ref
  43.0 2.5 %shard_map.103 = bf16[512,512]{1,0:T(8,128)(2,1)S(1)} custom-call(f32[40,128]{1,0:T(8,128)S(1)} %shard_map.102.own_ref, f32[40,128]{1,0:T(8,128)S(1)} %collective-permute-done.2.near_ref, f32[40,128]{1,0:T(8,128)S(1)} %collective-permute-done.3.far_ref, bf16[512,512]{1,0:T(8,128)(2,1)S(1)} %bitcast.22), custom_call_target="tpu_custom_call" | custom-call | tf_op jit(solution)/shard_map/pallas_call | solution.py:265
  45.6 21.8 %all_to_all.11 = bf16[32,16,512]{2,1,0:T(8,128)(2,1)S(1)} all-to-all(bf16[32,16,512]{2,1,0:T(8,128)(2,1)S(1)} %bitcast.23), channel_id=1, replica_groups=mesh['member'=32,'space'=8] {'member'}, dimensions={0} | all-to-all | bytes 1048576 | tf_op jit(solution)/shard_map/all_to_all | solution.py:326
  67.3 0.7 %shard_map.104 = bf16[2,4,80,360]{3,2,1,0:T(8,128)(2,1)S(1)} custom-call(bf16[512,512]{1,0:T(8,128)(2,1)S(1)} %bitcast.24), custom_call_target="tpu_custom_call" | custom-call | tf_op jit(solution)/shard_map/pallas_call | solution.py:265
  68.0 1.0 %copy.14 = bf16[2,80,4,360]{3,2,1,0:T(4,128)(2,1)} copy(bf16[2,80,4,360]{3,1,2,0:T(8,128)(2,1)S(1)} %bitcast.26) | data formatting | bytes 921600 | tf_op jit(solution)/shard_map/transpose | solution.py:336
  (12 shorter events, 0.1 us)
Async XLA Ops:
  1.2 6.2 %collective-permute-start.1 = (bf16[2,80,384]{2,1,0:T(8,128)(2,1)S(1)}, bf16[2,80,384]{2,1,0:T(8,128)(2,1)S(1)}, u32[]{:S(2)}, u32[]{:S(2)}) collective-permute-start(bf16[2,80,384]{2,1,0:T(8,128)(2,1)S(1)} %get-tuple-element.15), channel_id=1, source_target_pairs={{1,2},{2,1},{3,4},{4,3},{5,6},{6,5},{9,10},{10,9},{11,12},{12,11},... | collective-permute-start | bytes 368648 | tf_op jit(solution)/shard_map/ppermute | solution.py:291
  3.4 0.9 %copy-start = (bf16[1,80,320]{2,1,0:T(8,128)(2,1)S(1)}, bf16[1,80,320]{2,1,0:T(8,128)(2,1)}, u32[]{:S(2)}) copy-start(bf16[1,80,320]{2,1,0:T(8,128)(2,1)} %param.14) | copy-start | bytes 153604
  3.4 0.9 %copy-start.1 = (bf16[1,9,80,80]{3,2,1,0:T(8,128)(2,1)S(1)}, bf16[1,9,80,80]{3,2,1,0:T(8,128)(2,1)}, u32[]{:S(2)}) copy-start(bf16[1,9,80,80]{3,2,1,0:T(8,128)(2,1)} %conv.1) | copy-start | bytes 345604
  3.4 0.9 %copy-start.2 = (bf16[1,320,80]{1,2,0:T(8,128)(2,1)S(1)}, bf16[1,320,80]{1,2,0:T(8,128)(2,1)}, u32[]{:S(2)}) copy-start(bf16[1,320,80]{1,2,0:T(8,128)(2,1)} %param.13) | copy-start | bytes 153604
  3.4 4.0 %collective-permute-start = (bf16[2,80,384]{2,1,0:T(8,128)(2,1)S(1)}, bf16[2,80,384]{2,1,0:T(8,128)(2,1)S(1)}, u32[]{:S(2)}, u32[]{:S(2)}) collective-permute-start(bf16[2,80,384]{2,1,0:T(8,128)(2,1)S(1)} %get-tuple-element.16), channel_id=1, source_target_pairs={{0,1},{1,0},{2,3},{3,2},{4,5},{5,4},{6,7},{7,6},{8,9},{9,8},{10,11... | collective-permute-start | bytes 368648 | tf_op jit(solution)/shard_map/ppermute | solution.py:293
  3.5 0.8 %copy-start.4 = (s32[1,1,256]{2,1,0:T(1,128)S(1)}, s32[1,1,256]{2,1,0:T(1,128)}, u32[]{:S(2)}) copy-start(s32[1,1,256]{2,1,0:T(1,128)} %param.17) | copy-start | bytes 3076
  3.5 0.8 %copy-start.5 = (f32[1,1,256]{2,1,0:T(1,128)S(1)}, f32[1,1,256]{2,1,0:T(1,128)}, u32[]{:S(2)}) copy-start(f32[1,1,256]{2,1,0:T(1,128)} %param.18) | copy-start | bytes 3076
  3.5 0.8 %copy-start.6 = (f32[1,1,256]{2,1,0:T(1,128)S(1)}, f32[1,1,256]{2,1,0:T(1,128)}, u32[]{:S(2)}) copy-start(f32[1,1,256]{2,1,0:T(1,128)} %param.19) | copy-start | bytes 3076
  4.3 0.7 %copy-start.3 = (s32[1,1,256]{2,1,0:T(1,128)S(1)}, s32[1,1,256]{2,1,0:T(1,128)}, u32[]{:S(2)}) copy-start(s32[1,1,256]{2,1,0:T(1,128)} %param.16) | copy-start | bytes 3076
  4.3 0.7 %copy-start.7 = (f32[1,80]{1,0:T(1,128)S(1)}, f32[1,80]{1,0:T(1,128)}, u32[]{:S(2)}) copy-start(f32[1,80]{1,0:T(1,128)} %gain.1) | copy-start | bytes 964
  38.7 3.8 %collective-permute-start.3 = (f32[40,128]{1,0:T(8,128)S(1)}, f32[40,128]{1,0:T(8,128)S(1)}, u32[]{:S(2)}, u32[]{:S(2)}) collective-permute-start(f32[40,128]{1,0:T(8,128)S(1)} %shard_map.102.own_ref), channel_id=1, source_target_pairs={{0,248},{8,16},{16,8},{24,32},{32,24},{40,48},{48,40},{56,64},{64,... | collective-permute-start | bytes 61448 | tf_op jit(solution)/shard_map/ppermute | solution.py:332
  39.2 3.8 %collective-permute-start.2 = (f32[40,128]{1,0:T(8,128)S(1)}, f32[40,128]{1,0:T(8,128)S(1)}, u32[]{:S(2)}, u32[]{:S(2)}) collective-permute-start(f32[40,128]{1,0:T(8,128)S(1)} %shard_map.102.own_ref), channel_id=1, source_target_pairs={{0,8},{8,0},{16,24},{24,16},{32,40},{40,32},{48,56},{56,48},{64,72... | collective-permute-start | bytes 61448 | tf_op jit(solution)/shard_map/ppermute | solution.py:333

commit v4 on v3

--- a/solution.py
+++ b/solution.py
@@ -241,24 +241,30 @@
     out_ref[...] = mm(square, tile_ref[...]).astype(BF16)
 
 
-def unpack_kernel(in_ref, out_ref):
+def unpack_kernel(in_ref, out_hbm, laid, sent):
     spot = lax.broadcasted_iota(jnp.int32, (2 * SUB, 128), 1)
-
-    @pl.loop(0, ROWS)
-    def _(r):
-        for pair in range(SLOTS // 2):
+    copies = []
+    for pair in range(SLOTS // 2):
+        rows = []
+        for r in range(ROWS):
             lines = []
             for s in (2 * pair, 2 * pair + 1):
                 line = [jnp.zeros((2 * SUB, 128), F32) for _ in range(WIDE // 128)]
                 for j in range(PER_ROW):
-                    at = pl.multiple_of((r * PER_ROW + j) * 2 * SUB, 2 * SUB)
-                    for a, b, shift, start, stop in pieces(s * POINTS, j * POINTS, POINTS):
-                        both = in_ref[pl.ds(at, 2 * SUB), a * 128 : (a + 1) * 128].astype(F32)
-                        line[b] = jnp.where((spot >= start) & (spot < stop), move(both, shift), line[b])
+                    at = (r * PER_ROW + j) * 2 * SUB
+                    for a, b, shift, low, high in pieces(s * POINTS, j * POINTS, POINTS):
+                        both = in_ref[at : at + 2 * SUB, a * 128 : (a + 1) * 128].astype(F32)
+                        line[b] = jnp.where((spot >= low) & (spot < high), move(both, shift), line[b])
                 lines.append(jnp.concatenate(line, axis=1))
-            for m in range(2):
-                joined = jnp.concatenate([line[m * SUB : (m + 1) * SUB] for line in lines], axis=0)
-                out_ref[m, r, pair * 2 * SUB : (pair + 1) * 2 * SUB, :] = joined.astype(BF16)[:, :LON]
+            rows.append(lines)
+        block = slice(pair * 2 * SUB, (pair + 1) * 2 * SUB)
+        for m in range(2):
+            joined = [jnp.concatenate([line[m * SUB : (m + 1) * SUB] for line in lines], axis=0) for lines in rows]
+            laid[m, block] = jnp.swapaxes(jnp.stack(joined), 0, 1)[:, :, :LON].astype(BF16)
+        copies.append(pltpu.make_async_copy(laid.at[:, block], out_hbm.at[:, block], sent.at[pair]))
+        copies[-1].start()
+    for copy in copies:
+        copy.wait()
 
 
 def call(kernel, out_shape, *operands, **more):
@@ -332,8 +338,13 @@
     far = lax.ppermute(own, "member", [(i, (i + 1 if i % 2 else i - 1) % around) for i in range(around)])
     near = lax.ppermute(own, "member", [(i, i ^ 1) for i in range(around)])
     returned = exchange(call(blend_kernel, packed, own, near, far, tile))
-    result = call(unpack_kernel, jax.ShapeDtypeStruct((2, ROWS, CHANNELS, LON), BF16), returned)
-    return result.transpose(0, 2, 1, 3)
+    return call(
+        unpack_kernel,
+        jax.ShapeDtypeStruct((2, CHANNELS, ROWS, LON), BF16),
+        returned,
+        out_specs=pl.BlockSpec(memory_space=pl.ANY),
+        scratch_shapes=[pltpu.VMEM((2, CHANNELS, ROWS, LON), BF16), pltpu.SemaphoreType.DMA((SLOTS // 2,))],
+    )
 
 
 def solution(mesh):

time: 70.2 us -> 69.9 us (level)
  local copies, waits for them, and re-layouts: 2.87 us -> 1.9 us
    transpose x1 -> x0, local copies, waits for them, and re-layouts: 0.97 us -> none  [body(): return result.transpose(0, 2, 1, 3)]
    pallas_call x5, Pallas kernels: 7.56 us -> 8.26 us  [call(): pl.pallas_call(kernel, out_shape=out_shape, compiler_params=pltpu.Compile...]
where the time goes in v4:
time: 69.9 us; the launch traced here: 68.7 us
  blocking collectives  50.6 us (72%)
  Pallas kernels  8.26 us (12%)
  starting transfers between devices  4.64 us (7%)
  waiting for transfers between devices  2.47 us (4%)
  local copies, waits for them, and re-layouts  1.9 us (3%)
  between operations  0.79 us (1%)
    all_to_all x2, blocking collectives, exchange(): lax.all_to_all(block, 'member', split_axis=0, concat_axis=0, tiled=True)  50.6 us
    pallas_call x5, Pallas kernels, call(): pl.pallas_call(kernel, out_shape=out_shape, compiler_params=pltpu.Compile...  8.26 us
    ppermute x1, starting transfers between devices, body(): next_row = lax.ppermute(jnp.where(odd == 1, bottom, top), 'space', across)  2.18 us
    ppermute x1, starting transfers between devices, body(): near = lax.ppermute(own, 'member', [(i, i ^ 1) for i in range(around)])  1.86 us
    unnamed x17, local copies, waits for them, and re-layouts  1.8 us
    ppermute x1, waiting for transfers between devices, body(): lax.ppermute(own, 'member', [(i, (i + 1 if i % 2 else i - 1) % around) fo...  1.47 us
  transfers between devices with their start and end apart: 4, of which 3 were waited for; matrix products, arithmetic and copies ran while one was open for 0% of the time, Pallas kernels for 3%

profile of v4, /device:TPU:38, one launch (start us, length us, event | category | flops | bytes accessed | tf_op | source)
XLA Modules:
  0.0 68.7 jit_solution(18133708972715222287)
XLA Ops:
  0.0 1.1 %copy.15 = bf16[2,80,4,360]{3,1,0,2:T(8,128)(2,1)S(1)} copy(bf16[2,80,4,360]{3,2,1,0:T(4,128)(2,1)} %param.10) | data formatting | bytes 921600 | tf_op args[0]
  1.1 0.1 pad.4
  1.2 2.2 %collective-permute-start.1 = (bf16[2,80,384]{2,1,0:T(8,128)(2,1)S(1)}, bf16[2,80,384]{2,1,0:T(8,128)(2,1)S(1)}, u32[]{:S(2)}, u32[]{:S(2)}) collective-permute-start(bf16[2,80,384]{2,1,0:T(8,128)(2,1)S(1)} %get-tuple-element.15), channel_id=1, source_target_pairs={{1,2},{2,1},{3,4},{4,3},{5,6},{6,5},{9,10},{10,9},{11,12},{12,11},... | collective-permute-start | bytes 368648 | tf_op jit(solution)/shard_map/ppermute | solution.py:297
  3.4 0.0 copy-start.1
  3.4 0.0 copy-start.2
  3.4 0.1 collective-permute-start
  3.5 0.0 copy-start.5
  3.5 0.0 copy-start.6
  3.6 0.1 copy.13.x_ref
  4.3 0.0 copy-start.3
  4.3 0.0 copy-done.1
  4.4 0.6 copy-done.3
  5.0 1.9 %shard_map.100 = (bf16[256,512]{1,0:T(8,128)(2,1)S(1)}, bf16[240,240]{1,0:T(8,128)(2,1)S(1)}, f32[80,128]{1,0:T(8,128)S(1)}, bf16[320,80]{1,0:T(8,128)(2,1)S(1)}, f32[8,256]{1,0:T(8,128)S(1)}) custom-call(bf16[2,4,80,384]{3,2,1,0:T(8,128)(2,1)S(1)} %copy.13.x_ref, bf16[1,9,80,80]{3,2,1,0:T(8,128)(2,1)S(1)} %copy-done.1, f32[1,80]{1,0:T(1,128)S(1)} %copy-done.7, ...), custom_call_target="tpu_custom_call" | custom-call | flops 400000000 | bytes 2000000 | tf_op jit(solution)/shard_map/pallas_call | solution.py:271
  6.9 0.5 collective-permute-done.1.next_ref
  7.4 1.8 %shard_map.101 = bf16[512,512]{1,0:T(8,128)(2,1)S(1)} custom-call(s32[1,1]{1,0:T(1,128)} %bitcast.odd_ref, bf16[2,4,80,384]{3,2,1,0:T(8,128)(2,1)S(1)} %copy.13.x_ref, bf16[2,80,384]{2,1,0:T(8,128)(2,1)S(1)} %collective-permute-done.chip_ref, bf16[2,80,384]{2,1,0:T(8,128)(2,1)S(1)} %collective-permute-done.1.next_ref, ...), custom_call_target="tpu_custom_call" | custom-call | tf_op jit(solution)/shard_map/pallas_call | solution.py:271
  9.2 28.9 %all_to_all.10 = bf16[32,16,512]{2,1,0:T(8,128)(2,1)S(1)} all-to-all(bf16[32,16,512]{2,1,0:T(8,128)(2,1)S(1)} %bitcast.24), channel_id=1, replica_groups=mesh['member'=32,'space'=8] {'member'}, dimensions={0} | all-to-all | bytes 1048576 | tf_op jit(solution)/shard_map/all_to_all | solution.py:332
  38.1 0.6 shard_map.102.own_ref
  38.7 0.5 collective-permute-start.3
  39.2 1.9 %collective-permute-start.2 = (f32[40,128]{1,0:T(8,128)S(1)}, f32[40,128]{1,0:T(8,128)S(1)}, u32[]{:S(2)}, u32[]{:S(2)}) collective-permute-start(f32[40,128]{1,0:T(8,128)S(1)} %shard_map.102.own_ref), channel_id=1, source_target_pairs={{0,8},{8,0},{16,24},{24,16},{32,40},{40,32},{48,56},{56,48},{64,72... | collective-permute-start | bytes 61448 | tf_op jit(solution)/shard_map/ppermute | solution.py:339
  41.1 1.5 %collective-permute-done.3.far_ref = f32[40,128]{1,0:T(8,128)S(1)} collective-permute-done((f32[40,128]{1,0:T(8,128)S(1)}, f32[40,128]{1,0:T(8,128)S(1)}, u32[]{:S(2)}, u32[]{:S(2)}) %collective-permute-start.3) | collective-permute-done | bytes 20512 | tf_op jit(solution)/shard_map/ppermute | solution.py:338
  42.6 0.4 collective-permute-done.2.near_ref
  43.0 2.5 %shard_map.103 = bf16[512,512]{1,0:T(8,128)(2,1)S(1)} custom-call(f32[40,128]{1,0:T(8,128)S(1)} %shard_map.102.own_ref, f32[40,128]{1,0:T(8,128)S(1)} %collective-permute-done.2.near_ref, f32[40,128]{1,0:T(8,128)S(1)} %collective-permute-done.3.far_ref, bf16[512,512]{1,0:T(8,128)(2,1)S(1)} %bitcast.21), custom_call_target="tpu_custom_call" | custom-call | tf_op jit(solution)/shard_map/pallas_call | solution.py:271
  45.6 21.8 %all_to_all.11 = bf16[32,16,512]{2,1,0:T(8,128)(2,1)S(1)} all-to-all(bf16[32,16,512]{2,1,0:T(8,128)(2,1)S(1)} %bitcast.22), channel_id=1, replica_groups=mesh['member'=32,'space'=8] {'member'}, dimensions={0} | all-to-all | bytes 1048576 | tf_op jit(solution)/shard_map/all_to_all | solution.py:332
  67.3 1.4 %shard_map.104 = bf16[2,80,4,360]{3,2,1,0:T(4,128)(2,1)} custom-call(bf16[512,512]{1,0:T(8,128)(2,1)S(1)} %bitcast.23), custom_call_target="tpu_custom_call" | custom-call | tf_op jit(solution)/shard_map/pallas_call | solution.py:271
  (11 shorter events, 0.1 us)
Async XLA Ops:
  1.2 6.2 %collective-permute-start.1 = (bf16[2,80,384]{2,1,0:T(8,128)(2,1)S(1)}, bf16[2,80,384]{2,1,0:T(8,128)(2,1)S(1)}, u32[]{:S(2)}, u32[]{:S(2)}) collective-permute-start(bf16[2,80,384]{2,1,0:T(8,128)(2,1)S(1)} %get-tuple-element.15), channel_id=1, source_target_pairs={{1,2},{2,1},{3,4},{4,3},{5,6},{6,5},{9,10},{10,9},{11,12},{12,11},... | collective-permute-start | bytes 368648 | tf_op jit(solution)/shard_map/ppermute | solution.py:297
  3.4 0.9 %copy-start = (bf16[1,80,320]{2,1,0:T(8,128)(2,1)S(1)}, bf16[1,80,320]{2,1,0:T(8,128)(2,1)}, u32[]{:S(2)}) copy-start(bf16[1,80,320]{2,1,0:T(8,128)(2,1)} %param.14) | copy-start | bytes 153604
  3.4 0.9 %copy-start.1 = (bf16[1,9,80,80]{3,2,1,0:T(8,128)(2,1)S(1)}, bf16[1,9,80,80]{3,2,1,0:T(8,128)(2,1)}, u32[]{:S(2)}) copy-start(bf16[1,9,80,80]{3,2,1,0:T(8,128)(2,1)} %conv.1) | copy-start | bytes 345604
  3.4 0.9 %copy-start.2 = (bf16[1,320,80]{1,2,0:T(8,128)(2,1)S(1)}, bf16[1,320,80]{1,2,0:T(8,128)(2,1)}, u32[]{:S(2)}) copy-start(bf16[1,320,80]{1,2,0:T(8,128)(2,1)} %param.13) | copy-start | bytes 153604
  3.4 4.0 %collective-permute-start = (bf16[2,80,384]{2,1,0:T(8,128)(2,1)S(1)}, bf16[2,80,384]{2,1,0:T(8,128)(2,1)S(1)}, u32[]{:S(2)}, u32[]{:S(2)}) collective-permute-start(bf16[2,80,384]{2,1,0:T(8,128)(2,1)S(1)} %get-tuple-element.16), channel_id=1, source_target_pairs={{0,1},{1,0},{2,3},{3,2},{4,5},{5,4},{6,7},{7,6},{8,9},{9,8},{10,11... | collective-permute-start | bytes 368648 | tf_op jit(solution)/shard_map/ppermute | solution.py:299
  3.5 0.8 %copy-start.4 = (s32[1,1,256]{2,1,0:T(1,128)S(1)}, s32[1,1,256]{2,1,0:T(1,128)}, u32[]{:S(2)}) copy-start(s32[1,1,256]{2,1,0:T(1,128)} %param.17) | copy-start | bytes 3076
  3.5 0.8 %copy-start.5 = (f32[1,1,256]{2,1,0:T(1,128)S(1)}, f32[1,1,256]{2,1,0:T(1,128)}, u32[]{:S(2)}) copy-start(f32[1,1,256]{2,1,0:T(1,128)} %param.18) | copy-start | bytes 3076
  3.5 0.8 %copy-start.6 = (f32[1,1,256]{2,1,0:T(1,128)S(1)}, f32[1,1,256]{2,1,0:T(1,128)}, u32[]{:S(2)}) copy-start(f32[1,1,256]{2,1,0:T(1,128)} %param.19) | copy-start | bytes 3076
  4.3 0.7 %copy-start.3 = (s32[1,1,256]{2,1,0:T(1,128)S(1)}, s32[1,1,256]{2,1,0:T(1,128)}, u32[]{:S(2)}) copy-start(s32[1,1,256]{2,1,0:T(1,128)} %param.16) | copy-start | bytes 3076
  4.3 0.7 %copy-start.7 = (f32[1,80]{1,0:T(1,128)S(1)}, f32[1,80]{1,0:T(1,128)}, u32[]{:S(2)}) copy-start(f32[1,80]{1,0:T(1,128)} %gain.1) | copy-start | bytes 964
  38.7 3.8 %collective-permute-start.3 = (f32[40,128]{1,0:T(8,128)S(1)}, f32[40,128]{1,0:T(8,128)S(1)}, u32[]{:S(2)}, u32[]{:S(2)}) collective-permute-start(f32[40,128]{1,0:T(8,128)S(1)} %shard_map.102.own_ref), channel_id=1, source_target_pairs={{0,248},{8,16},{16,8},{24,32},{32,24},{40,48},{48,40},{56,64},{64,... | collective-permute-start | bytes 61448 | tf_op jit(solution)/shard_map/ppermute | solution.py:338
  39.2 3.8 %collective-permute-start.2 = (f32[40,128]{1,0:T(8,128)S(1)}, f32[40,128]{1,0:T(8,128)S(1)}, u32[]{:S(2)}, u32[]{:S(2)}) collective-permute-start(f32[40,128]{1,0:T(8,128)S(1)} %shard_map.102.own_ref), channel_id=1, source_target_pairs={{0,8},{8,0},{16,24},{24,16},{32,40},{40,32},{48,56},{56,48},{64,72... | collective-permute-start | bytes 61448 | tf_op jit(solution)/shard_map/ppermute | solution.py:339

commit v5 on v4

--- a/solution.py
+++ b/solution.py
@@ -15,6 +15,7 @@
 WIDE = 384
 POINTS = 45
 TILES = 32
+BANDS = 8
 PER_ROW = 8
 SUB = 8
 SLOTS = CHANNELS // SUB
@@ -73,32 +74,28 @@
     return here + west + east
 
 
-def forecast_rows(windows, conv_ref, gain_ref, first_ref, second_ref, held):
-    conv = conv_ref[...]
-    first = first_ref[...]
-    second = second_ref[...]
-    gain = gain_ref[:, :1]
+def convolve(windows, conv):
     lane = lax.broadcasted_iota(jnp.int32, (CHANNELS, 128), 1)
-    for m in range(2):
-        near, far = windows[m]
-        stacked = jnp.concatenate(
-            [jnp.concatenate([near[a], far[a]], axis=1) for a in range(3)], axis=0
-        )
-        taps = mm(conv, stacked)
-        parts = []
-        for d, window in enumerate(windows[m]):
-            west, here, east = [
-                taps[CHANNELS * b : CHANNELS * (b + 1), WIDE * d : WIDE * (d + 1)] for b in range(3)
-            ]
-            parts.append(window[1].astype(F32) + shift_wrapped(west, here, east, lane))
-        updated = jnp.concatenate(parts, axis=1)
-        power = jnp.sum(updated * updated, axis=0, keepdims=True) * (1.0 / CHANNELS)
-        normed = (updated * lax.rsqrt(power + EPSILON) * gain).astype(BF16)
-        hidden = mm(first, normed)
-        hidden = (hidden * (0.5 + 0.5 * jnp.tanh(0.5 * hidden))).astype(BF16)
-        result = updated + mm(second, hidden)
-        held[0, m] = result[:, :WIDE]
-        held[1, m] = result[:, WIDE:]
+    near, far = windows
+    stacked = jnp.concatenate([jnp.concatenate([near[a], far[a]], axis=1) for a in range(3)], axis=0)
+    taps = mm(conv, stacked)
+    parts = []
+    for d, window in enumerate(windows):
+        west, here, east = [
+            taps[CHANNELS * b : CHANNELS * (b + 1), WIDE * d : WIDE * (d + 1)] for b in range(3)
+        ]
+        parts.append(window[1].astype(F32) + shift_wrapped(west, here, east, lane))
+    return jnp.concatenate(parts, axis=1)
+
+
+def pointwise(updated, gain, first, second, held, m):
+    power = jnp.sum(updated * updated, axis=0, keepdims=True) * (1.0 / CHANNELS)
+    normed = (updated * lax.rsqrt(power + EPSILON) * gain).astype(BF16)
+    hidden = mm(first, normed)
+    hidden = (hidden * (0.5 + 0.5 * jnp.tanh(0.5 * hidden))).astype(BF16)
+    result = updated + mm(second, hidden)
+    held[0, m] = result[:, :WIDE]
+    held[1, m] = result[:, WIDE:]
 
 
 def pack_rows(held, starts, out_ref):
@@ -121,42 +118,59 @@
 def inner_kernel(
     x_ref,
     conv,
-    gain,
     first,
+    second_ref,
     count,
-    point,
-    channel,
-    value,
-    precision,
-    second_ref,
+    gain_hbm,
+    point_hbm,
+    channel_hbm,
+    value_hbm,
+    precision_hbm,
     out_ref,
     conv_ref,
     gain_ref,
     first_ref,
     obs_ref,
     held,
+    updated,
+    gain,
+    point,
+    channel,
+    value,
+    precision,
+    arrived,
 ):
+    moves = [(gain_hbm, gain), (point_hbm, point), (channel_hbm, channel)]
+    moves += [(value_hbm, value), (precision_hbm, precision)]
+    copies = [pltpu.make_async_copy(source, target, arrived.at[i]) for i, (source, target) in enumerate(moves)]
+    for copy in copies:
+        copy.start()
     conv_ref[...] = jnp.concatenate(
         [conv[0, 3 * a : 3 * a + 3].reshape(3 * CHANNELS, CHANNELS) for a in range(3)], axis=1
     )
+    first_ref[...] = first[...].astype(F32).T.astype(BF16)
+    for m in range(2):
+        updated[m] = convolve([[x_ref[m, r + d] for d in (-1, 0, 1)] for r in (1, 2)], conv_ref[...])
+    copies[0].wait()
     row = lax.broadcasted_iota(jnp.int32, (CHANNELS, CHANNELS), 0)
     column = lax.broadcasted_iota(jnp.int32, (CHANNELS, CHANNELS), 1)
     tall = jnp.sum(jnp.where(row == column, gain[...], 0.0), axis=1, keepdims=True)
     gain_ref[...] = jnp.broadcast_to(tall, (CHANNELS, 128))
-    first_ref[...] = first[...].astype(F32).T.astype(BF16)
+    for m in range(2):
+        pointwise(updated[m], gain_ref[:, :1], first_ref[...], second_ref[...], held, m)
+    pack_rows(held, (0, ROW_PACK), out_ref)
+    for copy in copies[1:]:
+        copy.wait()
     slots = lax.broadcasted_iota(jnp.int32, (1, OBS), 1)
     obs_ref[0:1, :] = ((channel[...] // SUB) * POINTS + point[...]).astype(F32)
     obs_ref[1:2, :] = (channel[...] % SUB).astype(F32)
     obs_ref[2:3, :] = jnp.where(slots < count[...], precision[...], 0.0)
     obs_ref[3:4, :] = value[...]
     obs_ref[4:, :] = jnp.zeros((4, OBS), F32)
-    windows = [[[x_ref[m, r + d] for d in (-1, 0, 1)] for r in (1, 2)] for m in range(2)]
-    forecast_rows(windows, conv_ref, gain_ref, first_ref, second_ref, held)
-    pack_rows(held, (0, ROW_PACK), out_ref)
 
 
 def outer_kernel(
-    odd_ref,
+    band_ref,
     x_ref,
     chip_ref,
     next_ref,
@@ -168,13 +182,18 @@
     out_ref,
     held,
 ):
-    odd = odd_ref[...] == 1
+    band = band_ref[...]
+    odd = band % 2 == 1
     windows = []
     for m in range(2):
-        low = jnp.where(odd, chip_ref[m].astype(F32), next_ref[m].astype(F32)).astype(BF16)
-        high = jnp.where(odd, next_ref[m].astype(F32), chip_ref[m].astype(F32)).astype(BF16)
+        chip = chip_ref[m].astype(F32)
+        beyond = next_ref[m].astype(F32)
+        low = jnp.where(band == 0, 0.0, jnp.where(odd, chip, beyond)).astype(BF16)
+        high = jnp.where(band == BANDS - 1, 0.0, jnp.where(odd, beyond, chip)).astype(BF16)
         windows.append([[low, x_ref[m, 0], x_ref[m, 1]], [x_ref[m, 2], x_ref[m, 3], high]])
-    forecast_rows(windows, conv_ref, gain_ref, first_ref, second_ref, held)
+    for m in range(2):
+        updated = convolve(windows[m], conv_ref[...])
+        pointwise(updated, gain_ref[:, :1], first_ref[...], second_ref[...], held, m)
     pack_rows(held, (0, 3 * ROW_PACK), out_ref)
     out_ref[ROW_PACK : 3 * ROW_PACK, :] = inner_ref[...]
 
@@ -290,15 +309,22 @@
 ):
     fields = jnp.pad(starting_fields.transpose(0, 2, 1, 3), ((0, 0), (0, 0), (0, 0), (0, WIDE - LON)))
     fields = lax.optimization_barrier(fields)
-    bands = lax.axis_size("space")
-    odd = lax.axis_index("space") % 2
+    band = lax.axis_index("space")
+    odd = band % 2
     top, bottom = fields[:, 0], fields[:, ROWS - 1]
-    across = [(i, i + 1 if i % 2 else i - 1) for i in range(1, bands - 1)]
+    across = [(i, (i + 1 if i % 2 else i - 1) % BANDS) for i in range(BANDS)]
     next_row = lax.ppermute(jnp.where(odd == 1, bottom, top), "space", across)
-    within = [(i, i ^ 1) for i in range(bands)]
+    within = [(i, i ^ 1) for i in range(BANDS)]
     chip_row = lax.ppermute(jnp.where(odd == 1, top, bottom), "space", within)
     held = [pltpu.VMEM((2, 2, CHANNELS, WIDE), F32)]
     second = weight_out[0]
+    small = [
+        (norm_gain, F32, (1, CHANNELS)),
+        (obs_point[0], jnp.int32, (1, OBS)),
+        (obs_channel[0], jnp.int32, (1, OBS)),
+        (obs_value[0], F32, (1, OBS)),
+        (obs_precision[0], F32, (1, OBS)),
+    ]
     inner, conv, gain, first, observations = call(
         inner_kernel,
         (
@@ -310,21 +336,21 @@
         ),
         fields,
         conv_weight,
-        norm_gain,
         weight_in[0].T,
+        second,
         obs_count,
-        obs_point[0],
-        obs_channel[0],
-        obs_value[0],
-        obs_precision[0],
-        second,
-        scratch_shapes=held,
+        *[pltpu.with_memory_space_constraint(array, pltpu.HBM) for array, _, _ in small],
+        in_specs=[pl.BlockSpec(memory_space=pltpu.VMEM)] * 5 + [pl.BlockSpec(memory_space=pltpu.HBM)] * 5,
+        scratch_shapes=held
+        + [pltpu.VMEM((2, CHANNELS, 2 * WIDE), F32)]
+        + [pltpu.VMEM(shape, kind) for _, kind, shape in small]
+        + [pltpu.SemaphoreType.DMA((len(small),))],
         cost_estimate=pl.CostEstimate(flops=400_000_000, bytes_accessed=2_000_000, transcendentals=500_000),
     )
     weights = (conv, gain, first, second)
     packed = jax.ShapeDtypeStruct((PACK, PACK), BF16)
     sent = call(
-        outer_kernel, packed, odd.reshape(1, 1), fields, chip_row, next_row, inner, *weights, scratch_shapes=held
+        outer_kernel, packed, band.reshape(1, 1), fields, chip_row, next_row, inner, *weights, scratch_shapes=held
     )
 
     def exchange(block):

time: 69.9 us -> 69.8 us (level); the launches traced: 68.7 us -> 69.6 us
  blocking collectives: 50.6 us -> 53.2 us
  starting transfers between devices: 4.64 us -> 3.28 us
    all_to_all x2, blocking collectives: 50.6 us -> 53.2 us  [exchange(): lax.all_to_all(block, 'member', split_axis=0, concat_axis=0, tiled=True)]
    ppermute x1, starting transfers between devices: 2.18 us -> 0.35 us  [body(): next_row = lax.ppermute(jnp.where(odd == 1, bottom, top), 'space', across)]
    unnamed x17 -> x7, local copies, waits for them, and re-layouts: 1.8 us -> 1.1 us
where the time goes in v5:
time: 69.8 us; the launch traced here: 69.6 us
  blocking collectives  53.2 us (76%)
  Pallas kernels  8.45 us (12%)
  starting transfers between devices  3.28 us (5%)
  waiting for transfers between devices  2.66 us (4%)
  local copies, waits for them, and re-layouts  1.21 us (2%)
  between operations  0.72 us (1%)
    all_to_all x2, blocking collectives, exchange(): lax.all_to_all(block, 'member', split_axis=0, concat_axis=0, tiled=True)  53.2 us
    pallas_call x5, Pallas kernels, call(): pl.pallas_call(kernel, out_shape=out_shape, compiler_params=pltpu.Compile...  8.45 us
    ppermute x1, starting transfers between devices, body(): near = lax.ppermute(own, 'member', [(i, i ^ 1) for i in range(around)])  2.4 us
  transfers between devices with their start and end apart: 4, of which 3 were waited for; matrix products, arithmetic and copies ran while one was open for 0% of the time, Pallas kernels for 3%

profile of v5, /device:TPU:38, one launch (start us, length us, event | category | flops | bytes accessed | tf_op | source)
XLA Modules:
  0.0 69.6 jit_solution(735190761860414683)
XLA Ops:
  0.0 1.1 %copy.15 = bf16[2,80,4,360]{3,1,0,2:T(8,128)(2,1)S(1)} copy(bf16[2,80,4,360]{3,2,1,0:T(4,128)(2,1)} %param.10) | data formatting | bytes 921600 | tf_op args[0]
  1.1 0.1 pad.4
  1.2 0.4 collective-permute-start.1
  1.6 0.0 copy-start
  1.6 0.0 copy-start.1
  1.6 0.0 copy-start.2
  1.6 0.3 collective-permute-start
  1.9 0.1 copy.13.x_ref
  2.6 0.0 copy-done
  2.6 0.0 copy-done.1
  2.6 0.0 copy-done.2
  2.6 2.1 %shard_map.100 = (bf16[256,512]{1,0:T(8,128)(2,1)S(1)}, bf16[240,240]{1,0:T(8,128)(2,1)S(1)}, f32[80,128]{1,0:T(8,128)S(1)}, bf16[320,80]{1,0:T(8,128)(2,1)S(1)}, f32[8,256]{1,0:T(8,128)S(1)}) custom-call(bf16[2,4,80,384]{3,2,1,0:T(8,128)(2,1)S(1)} %copy.13.x_ref, bf16[1,9,80,80]{3,2,1,0:T(8,128)(2,1)S(1)} %copy-done.1, bf16[80,320]{1,0:T(8,128)(2,1)S(1)} %bitcast.27, ...), custom_call_target="tpu_custom_call" | custom-call | flops 400000000 | bytes 2000000 | tf_op jit(solution)/shard_map/pallas_call | solution.py:290
  4.7 0.9 %collective-permute-done.1.next_ref = bf16[2,80,384]{2,1,0:T(8,128)(2,1)S(1)} collective-permute-done((bf16[2,80,384]{2,1,0:T(8,128)(2,1)S(1)}, bf16[2,80,384]{2,1,0:T(8,128)(2,1)S(1)}, u32[]{:S(2)}, u32[]{:S(2)}) %collective-permute-start.1) | collective-permute-done | bytes 122912 | tf_op jit(solution)/shard_map/ppermute | solution.py:316
  5.6 0.0 collective-permute-done.chip_ref
  5.6 1.8 %shard_map.101 = bf16[512,512]{1,0:T(8,128)(2,1)S(1)} custom-call(s32[1,1]{1,0:T(1,128)} %bitcast.band_ref, bf16[2,4,80,384]{3,2,1,0:T(8,128)(2,1)S(1)} %copy.13.x_ref, bf16[2,80,384]{2,1,0:T(8,128)(2,1)S(1)} %collective-permute-done.chip_ref, bf16[2,80,384]{2,1,0:T(8,128)(2,1)S(1)} %collective-permute-done.1.next_ref, ...), custom_call_target="tpu_custom_call" | custom-call | tf_op jit(solution)/shard_map/pallas_call | solution.py:290
  7.4 29.8 %all_to_all.10 = bf16[32,16,512]{2,1,0:T(8,128)(2,1)S(1)} all-to-all(bf16[32,16,512]{2,1,0:T(8,128)(2,1)S(1)} %bitcast.24), channel_id=1, replica_groups=mesh['member'=32,'space'=8] {'member'}, dimensions={0} | all-to-all | bytes 1048576 | tf_op jit(solution)/shard_map/all_to_all | solution.py:358
  37.2 0.6 shard_map.102.own_ref
  37.8 0.2 collective-permute-start.3
  38.0 2.4 %collective-permute-start.2 = (f32[40,128]{1,0:T(8,128)S(1)}, f32[40,128]{1,0:T(8,128)S(1)}, u32[]{:S(2)}, u32[]{:S(2)}) collective-permute-start(f32[40,128]{1,0:T(8,128)S(1)} %shard_map.102.own_ref), channel_id=1, source_target_pairs={{0,8},{8,0},{16,24},{24,16},{32,40},{40,32},{48,56},{56,48},{64,72... | collective-permute-start | bytes 61448 | tf_op jit(solution)/shard_map/ppermute | solution.py:365
  40.5 1.2 %collective-permute-done.3.far_ref = f32[40,128]{1,0:T(8,128)S(1)} collective-permute-done((f32[40,128]{1,0:T(8,128)S(1)}, f32[40,128]{1,0:T(8,128)S(1)}, u32[]{:S(2)}, u32[]{:S(2)}) %collective-permute-start.3) | collective-permute-done | bytes 20512 | tf_op jit(solution)/shard_map/ppermute | solution.py:364
  41.7 0.5 collective-permute-done.2.near_ref
  42.2 2.5 %shard_map.103 = bf16[512,512]{1,0:T(8,128)(2,1)S(1)} custom-call(f32[40,128]{1,0:T(8,128)S(1)} %shard_map.102.own_ref, f32[40,128]{1,0:T(8,128)S(1)} %collective-permute-done.2.near_ref, f32[40,128]{1,0:T(8,128)S(1)} %collective-permute-done.3.far_ref, bf16[512,512]{1,0:T(8,128)(2,1)S(1)} %bitcast.21), custom_call_target="tpu_custom_call" | custom-call | tf_op jit(solution)/shard_map/pallas_call | solution.py:290
  44.8 23.4 %all_to_all.11 = bf16[32,16,512]{2,1,0:T(8,128)(2,1)S(1)} all-to-all(bf16[32,16,512]{2,1,0:T(8,128)(2,1)S(1)} %bitcast.22), channel_id=1, replica_groups=mesh['member'=32,'space'=8] {'member'}, dimensions={0} | all-to-all | bytes 1048576 | tf_op jit(solution)/shard_map/all_to_all | solution.py:358
  68.2 1.4 %shard_map.104 = bf16[2,80,4,360]{3,2,1,0:T(4,128)(2,1)} custom-call(bf16[512,512]{1,0:T(8,128)(2,1)S(1)} %bitcast.23), custom_call_target="tpu_custom_call" | custom-call | tf_op jit(solution)/shard_map/pallas_call | solution.py:290
  (1 shorter events, 0.0 us)
Async XLA Ops:
  1.2 4.4 %collective-permute-start.1 = (bf16[2,80,384]{2,1,0:T(8,128)(2,1)S(1)}, bf16[2,80,384]{2,1,0:T(8,128)(2,1)S(1)}, u32[]{:S(2)}, u32[]{:S(2)}) collective-permute-start(bf16[2,80,384]{2,1,0:T(8,128)(2,1)S(1)} %get-tuple-element.15), channel_id=1, source_target_pairs={{0,7},{1,2},{2,1},{3,4},{4,3},{5,6},{6,5},{7,0},{8,15},{9,10},{10,... | collective-permute-start | bytes 368648 | tf_op jit(solution)/shard_map/ppermute | solution.py:316
  1.6 1.0 %copy-start = (bf16[1,80,320]{2,1,0:T(8,128)(2,1)S(1)}, bf16[1,80,320]{2,1,0:T(8,128)(2,1)}, u32[]{:S(2)}) copy-start(bf16[1,80,320]{2,1,0:T(8,128)(2,1)} %param.14) | copy-start | bytes 153604
  1.6 1.0 %copy-start.1 = (bf16[1,9,80,80]{3,2,1,0:T(8,128)(2,1)S(1)}, bf16[1,9,80,80]{3,2,1,0:T(8,128)(2,1)}, u32[]{:S(2)}) copy-start(bf16[1,9,80,80]{3,2,1,0:T(8,128)(2,1)} %conv.1) | copy-start | bytes 345604
  1.6 1.1 %copy-start.2 = (bf16[1,320,80]{1,2,0:T(8,128)(2,1)S(1)}, bf16[1,320,80]{1,2,0:T(8,128)(2,1)}, u32[]{:S(2)}) copy-start(bf16[1,320,80]{1,2,0:T(8,128)(2,1)} %param.13) | copy-start | bytes 153604
  1.6 4.0 %collective-permute-start = (bf16[2,80,384]{2,1,0:T(8,128)(2,1)S(1)}, bf16[2,80,384]{2,1,0:T(8,128)(2,1)S(1)}, u32[]{:S(2)}, u32[]{:S(2)}) collective-permute-start(bf16[2,80,384]{2,1,0:T(8,128)(2,1)S(1)} %get-tuple-element.16), channel_id=1, source_target_pairs={{0,1},{1,0},{2,3},{3,2},{4,5},{5,4},{6,7},{7,6},{8,9},{9,8},{10,11... | collective-permute-start | bytes 368648 | tf_op jit(solution)/shard_map/ppermute | solution.py:318
  37.8 3.8 %collective-permute-start.3 = (f32[40,128]{1,0:T(8,128)S(1)}, f32[40,128]{1,0:T(8,128)S(1)}, u32[]{:S(2)}, u32[]{:S(2)}) collective-permute-start(f32[40,128]{1,0:T(8,128)S(1)} %shard_map.102.own_ref), channel_id=1, source_target_pairs={{0,248},{8,16},{16,8},{24,32},{32,24},{40,48},{48,40},{56,64},{64,... | collective-permute-start | bytes 61448 | tf_op jit(solution)/shard_map/ppermute | solution.py:364
  38.0 4.2 %collective-permute-start.2 = (f32[40,128]{1,0:T(8,128)S(1)}, f32[40,128]{1,0:T(8,128)S(1)}, u32[]{:S(2)}, u32[]{:S(2)}) collective-permute-start(f32[40,128]{1,0:T(8,128)S(1)} %shard_map.102.own_ref), channel_id=1, source_target_pairs={{0,8},{8,0},{16,24},{24,16},{32,40},{40,32},{48,56},{56,48},{64,72... | collective-permute-start | bytes 61448 | tf_op jit(solution)/shard_map/ppermute | solution.py:365

commit v6 on v5

--- a/solution.py
+++ b/solution.py
@@ -74,28 +74,34 @@
     return here + west + east
 
 
-def convolve(windows, conv):
+def forecast_rows(windows, conv_ref, gain_ref, first_ref, second_ref, held, ready=None):
+    conv = conv_ref[...]
+    first = first_ref[...]
+    second = second_ref[...]
     lane = lax.broadcasted_iota(jnp.int32, (CHANNELS, 128), 1)
-    near, far = windows
-    stacked = jnp.concatenate([jnp.concatenate([near[a], far[a]], axis=1) for a in range(3)], axis=0)
-    taps = mm(conv, stacked)
-    parts = []
-    for d, window in enumerate(windows):
-        west, here, east = [
-            taps[CHANNELS * b : CHANNELS * (b + 1), WIDE * d : WIDE * (d + 1)] for b in range(3)
-        ]
-        parts.append(window[1].astype(F32) + shift_wrapped(west, here, east, lane))
-    return jnp.concatenate(parts, axis=1)
-
-
-def pointwise(updated, gain, first, second, held, m):
-    power = jnp.sum(updated * updated, axis=0, keepdims=True) * (1.0 / CHANNELS)
-    normed = (updated * lax.rsqrt(power + EPSILON) * gain).astype(BF16)
-    hidden = mm(first, normed)
-    hidden = (hidden * (0.5 + 0.5 * jnp.tanh(0.5 * hidden))).astype(BF16)
-    result = updated + mm(second, hidden)
-    held[0, m] = result[:, :WIDE]
-    held[1, m] = result[:, WIDE:]
+    for m in range(2):
+        near, far = windows[m]
+        stacked = jnp.concatenate(
+            [jnp.concatenate([near[a], far[a]], axis=1) for a in range(3)], axis=0
+        )
+        taps = mm(conv, stacked)
+        parts = []
+        for d, window in enumerate(windows[m]):
+            west, here, east = [
+                taps[CHANNELS * b : CHANNELS * (b + 1), WIDE * d : WIDE * (d + 1)] for b in range(3)
+            ]
+            parts.append(window[1].astype(F32) + shift_wrapped(west, here, east, lane))
+        updated = jnp.concatenate(parts, axis=1)
+        if ready is not None and m == 0:
+            ready()
+        gain = gain_ref[:, :1]
+        power = jnp.sum(updated * updated, axis=0, keepdims=True) * (1.0 / CHANNELS)
+        normed = (updated * lax.rsqrt(power + EPSILON) * gain).astype(BF16)
+        hidden = mm(first, normed)
+        hidden = (hidden * (0.5 + 0.5 * jnp.tanh(0.5 * hidden))).astype(BF16)
+        result = updated + mm(second, hidden)
+        held[0, m] = result[:, :WIDE]
+        held[1, m] = result[:, WIDE:]
 
 
 def pack_rows(held, starts, out_ref):
@@ -132,7 +138,6 @@
     first_ref,
     obs_ref,
     held,
-    updated,
     gain,
     point,
     channel,
@@ -149,24 +154,24 @@
         [conv[0, 3 * a : 3 * a + 3].reshape(3 * CHANNELS, CHANNELS) for a in range(3)], axis=1
     )
     first_ref[...] = first[...].astype(F32).T.astype(BF16)
-    for m in range(2):
-        updated[m] = convolve([[x_ref[m, r + d] for d in (-1, 0, 1)] for r in (1, 2)], conv_ref[...])
-    copies[0].wait()
-    row = lax.broadcasted_iota(jnp.int32, (CHANNELS, CHANNELS), 0)
-    column = lax.broadcasted_iota(jnp.int32, (CHANNELS, CHANNELS), 1)
-    tall = jnp.sum(jnp.where(row == column, gain[...], 0.0), axis=1, keepdims=True)
-    gain_ref[...] = jnp.broadcast_to(tall, (CHANNELS, 128))
-    for m in range(2):
-        pointwise(updated[m], gain_ref[:, :1], first_ref[...], second_ref[...], held, m)
+
+    def ready():
+        for copy in copies:
+            copy.wait()
+        row = lax.broadcasted_iota(jnp.int32, (CHANNELS, CHANNELS), 0)
+        column = lax.broadcasted_iota(jnp.int32, (CHANNELS, CHANNELS), 1)
+        tall = jnp.sum(jnp.where(row == column, gain[...], 0.0), axis=1, keepdims=True)
+        gain_ref[...] = jnp.broadcast_to(tall, (CHANNELS, 128))
+        slots = lax.broadcasted_iota(jnp.int32, (1, OBS), 1)
+        obs_ref[0:1, :] = ((channel[...] // SUB) * POINTS + point[...]).astype(F32)
+        obs_ref[1:2, :] = (channel[...] % SUB).astype(F32)
+        obs_ref[2:3, :] = jnp.where(slots < count[...], precision[...], 0.0)
+        obs_ref[3:4, :] = value[...]
+        obs_ref[4:, :] = jnp.zeros((4, OBS), F32)
+
+    windows = [[[x_ref[m, r + d] for d in (-1, 0, 1)] for r in (1, 2)] for m in range(2)]
+    forecast_rows(windows, conv_ref, gain_ref, first_ref, second_ref, held, ready)
     pack_rows(held, (0, ROW_PACK), out_ref)
-    for copy in copies[1:]:
-        copy.wait()
-    slots = lax.broadcasted_iota(jnp.int32, (1, OBS), 1)
-    obs_ref[0:1, :] = ((channel[...] // SUB) * POINTS + point[...]).astype(F32)
-    obs_ref[1:2, :] = (channel[...] % SUB).astype(F32)
-    obs_ref[2:3, :] = jnp.where(slots < count[...], precision[...], 0.0)
-    obs_ref[3:4, :] = value[...]
-    obs_ref[4:, :] = jnp.zeros((4, OBS), F32)
 
 
 def outer_kernel(
@@ -191,9 +196,7 @@
         low = jnp.where(band == 0, 0.0, jnp.where(odd, chip, beyond)).astype(BF16)
         high = jnp.where(band == BANDS - 1, 0.0, jnp.where(odd, beyond, chip)).astype(BF16)
         windows.append([[low, x_ref[m, 0], x_ref[m, 1]], [x_ref[m, 2], x_ref[m, 3], high]])
-    for m in range(2):
-        updated = convolve(windows[m], conv_ref[...])
-        pointwise(updated, gain_ref[:, :1], first_ref[...], second_ref[...], held, m)
+    forecast_rows(windows, conv_ref, gain_ref, first_ref, second_ref, held)
     pack_rows(held, (0, 3 * ROW_PACK), out_ref)
     out_ref[ROW_PACK : 3 * ROW_PACK, :] = inner_ref[...]
 
@@ -342,7 +345,6 @@
         *[pltpu.with_memory_space_constraint(array, pltpu.HBM) for array, _, _ in small],
         in_specs=[pl.BlockSpec(memory_space=pltpu.VMEM)] * 5 + [pl.BlockSpec(memory_space=pltpu.HBM)] * 5,
         scratch_shapes=held
-        + [pltpu.VMEM((2, CHANNELS, 2 * WIDE), F32)]
         + [pltpu.VMEM(shape, kind) for _, kind, shape in small]
         + [pltpu.SemaphoreType.DMA((len(small),))],
         cost_estimate=pl.CostEstimate(flops=400_000_000, bytes_accessed=2_000_000, transcendentals=500_000),

time: 69.8 us -> 69.8 us (level)
  transfers between devices with their start and end apart: 4 -> 4, of which waited for: 3 -> 3; matrix products, arithmetic and copies ran while one was open for 0% -> 0% of each run, Pallas kernels for 3% -> 4%
where the time goes in v6:
time: 69.8 us; the launch traced here: 69.6 us
  blocking collectives  53.2 us (76%)
  Pallas kernels  8.88 us (13%)
  starting transfers between devices  3.28 us (5%)
  waiting for transfers between devices  2.22 us (3%)
  local copies, waits for them, and re-layouts  1.21 us (2%)
  between operations  0.72 us (1%)
    all_to_all x2, blocking collectives, exchange(): lax.all_to_all(block, 'member', split_axis=0, concat_axis=0, tiled=True)  53.2 us
    pallas_call x5, Pallas kernels, call(): pl.pallas_call(kernel, out_shape=out_shape, compiler_params=pltpu.Compile...  8.88 us
    ppermute x1, starting transfers between devices, body(): near = lax.ppermute(own, 'member', [(i, i ^ 1) for i in range(around)])  2.4 us
  transfers between devices with their start and end apart: 4, of which 3 were waited for; matrix products, arithmetic and copies ran while one was open for 0% of the time, Pallas kernels for 4%

profile of v6, /device:TPU:38, one launch (start us, length us, event | category | flops | bytes accessed | tf_op | source)
XLA Modules:
  0.0 69.6 jit_solution(6136993761488526203)
XLA Ops:
  0.0 1.1 %copy.15 = bf16[2,80,4,360]{3,1,0,2:T(8,128)(2,1)S(1)} copy(bf16[2,80,4,360]{3,2,1,0:T(4,128)(2,1)} %param.10) | data formatting | bytes 921600 | tf_op args[0]
  1.1 0.1 pad.4
  1.2 0.4 collective-permute-start.1
  1.6 0.0 copy-start
  1.6 0.0 copy-start.1
  1.6 0.0 copy-start.2
  1.6 0.3 collective-permute-start
  1.9 0.1 copy.13.x_ref
  2.6 0.0 copy-done
  2.6 0.0 copy-done.1
  2.6 0.0 copy-done.2
  2.6 2.5 %shard_map.100 = (bf16[256,512]{1,0:T(8,128)(2,1)S(1)}, bf16[240,240]{1,0:T(8,128)(2,1)S(1)}, f32[80,128]{1,0:T(8,128)S(1)}, bf16[320,80]{1,0:T(8,128)(2,1)S(1)}, f32[8,256]{1,0:T(8,128)S(1)}) custom-call(bf16[2,4,80,384]{3,2,1,0:T(8,128)(2,1)S(1)} %copy.13.x_ref, bf16[1,9,80,80]{3,2,1,0:T(8,128)(2,1)S(1)} %copy-done.1, bf16[80,320]{1,0:T(8,128)(2,1)S(1)} %bitcast.27, ...), custom_call_target="tpu_custom_call" | custom-call | flops 400000000 | bytes 2000000 | tf_op jit(solution)/shard_map/pallas_call | solution.py:293
  5.1 0.5 collective-permute-done.1.next_ref
  5.6 0.0 collective-permute-done.chip_ref
  5.6 1.8 %shard_map.101 = bf16[512,512]{1,0:T(8,128)(2,1)S(1)} custom-call(s32[1,1]{1,0:T(1,128)} %bitcast.band_ref, bf16[2,4,80,384]{3,2,1,0:T(8,128)(2,1)S(1)} %copy.13.x_ref, bf16[2,80,384]{2,1,0:T(8,128)(2,1)S(1)} %collective-permute-done.chip_ref, bf16[2,80,384]{2,1,0:T(8,128)(2,1)S(1)} %collective-permute-done.1.next_ref, ...), custom_call_target="tpu_custom_call" | custom-call | tf_op jit(solution)/shard_map/pallas_call | solution.py:293
  7.4 29.8 %all_to_all.10 = bf16[32,16,512]{2,1,0:T(8,128)(2,1)S(1)} all-to-all(bf16[32,16,512]{2,1,0:T(8,128)(2,1)S(1)} %bitcast.24), channel_id=1, replica_groups=mesh['member'=32,'space'=8] {'member'}, dimensions={0} | all-to-all | bytes 1048576 | tf_op jit(solution)/shard_map/all_to_all | solution.py:360
  37.2 0.6 shard_map.102.own_ref
  37.8 0.2 collective-permute-start.3
  38.0 2.4 %collective-permute-start.2 = (f32[40,128]{1,0:T(8,128)S(1)}, f32[40,128]{1,0:T(8,128)S(1)}, u32[]{:S(2)}, u32[]{:S(2)}) collective-permute-start(f32[40,128]{1,0:T(8,128)S(1)} %shard_map.102.own_ref), channel_id=1, source_target_pairs={{0,8},{8,0},{16,24},{24,16},{32,40},{40,32},{48,56},{56,48},{64,72... | collective-permute-start | bytes 61448 | tf_op jit(solution)/shard_map/ppermute | solution.py:367
  40.4 1.2 %collective-permute-done.3.far_ref = f32[40,128]{1,0:T(8,128)S(1)} collective-permute-done((f32[40,128]{1,0:T(8,128)S(1)}, f32[40,128]{1,0:T(8,128)S(1)}, u32[]{:S(2)}, u32[]{:S(2)}) %collective-permute-start.3) | collective-permute-done | bytes 20512 | tf_op jit(solution)/shard_map/ppermute | solution.py:366
  41.7 0.5 collective-permute-done.2.near_ref
  42.2 2.5 %shard_map.103 = bf16[512,512]{1,0:T(8,128)(2,1)S(1)} custom-call(f32[40,128]{1,0:T(8,128)S(1)} %shard_map.102.own_ref, f32[40,128]{1,0:T(8,128)S(1)} %collective-permute-done.2.near_ref, f32[40,128]{1,0:T(8,128)S(1)} %collective-permute-done.3.far_ref, bf16[512,512]{1,0:T(8,128)(2,1)S(1)} %bitcast.21), custom_call_target="tpu_custom_call" | custom-call | tf_op jit(solution)/shard_map/pallas_call | solution.py:293
  44.8 23.4 %all_to_all.11 = bf16[32,16,512]{2,1,0:T(8,128)(2,1)S(1)} all-to-all(bf16[32,16,512]{2,1,0:T(8,128)(2,1)S(1)} %bitcast.22), channel_id=1, replica_groups=mesh['member'=32,'space'=8] {'member'}, dimensions={0} | all-to-all | bytes 1048576 | tf_op jit(solution)/shard_map/all_to_all | solution.py:360
  68.2 1.4 %shard_map.104 = bf16[2,80,4,360]{3,2,1,0:T(4,128)(2,1)} custom-call(bf16[512,512]{1,0:T(8,128)(2,1)S(1)} %bitcast.23), custom_call_target="tpu_custom_call" | custom-call | tf_op jit(solution)/shard_map/pallas_call | solution.py:293
  (1 shorter events, 0.0 us)
Async XLA Ops:
  1.2 4.4 %collective-permute-start.1 = (bf16[2,80,384]{2,1,0:T(8,128)(2,1)S(1)}, bf16[2,80,384]{2,1,0:T(8,128)(2,1)S(1)}, u32[]{:S(2)}, u32[]{:S(2)}) collective-permute-start(bf16[2,80,384]{2,1,0:T(8,128)(2,1)S(1)} %get-tuple-element.15), channel_id=1, source_target_pairs={{0,7},{1,2},{2,1},{3,4},{4,3},{5,6},{6,5},{7,0},{8,15},{9,10},{10,... | collective-permute-start | bytes 368648 | tf_op jit(solution)/shard_map/ppermute | solution.py:319
  1.6 1.0 %copy-start = (bf16[1,80,320]{2,1,0:T(8,128)(2,1)S(1)}, bf16[1,80,320]{2,1,0:T(8,128)(2,1)}, u32[]{:S(2)}) copy-start(bf16[1,80,320]{2,1,0:T(8,128)(2,1)} %param.14) | copy-start | bytes 153604
  1.6 1.0 %copy-start.1 = (bf16[1,9,80,80]{3,2,1,0:T(8,128)(2,1)S(1)}, bf16[1,9,80,80]{3,2,1,0:T(8,128)(2,1)}, u32[]{:S(2)}) copy-start(bf16[1,9,80,80]{3,2,1,0:T(8,128)(2,1)} %conv.1) | copy-start | bytes 345604
  1.6 1.1 %copy-start.2 = (bf16[1,320,80]{1,2,0:T(8,128)(2,1)S(1)}, bf16[1,320,80]{1,2,0:T(8,128)(2,1)}, u32[]{:S(2)}) copy-start(bf16[1,320,80]{1,2,0:T(8,128)(2,1)} %param.13) | copy-start | bytes 153604
  1.6 4.0 %collective-permute-start = (bf16[2,80,384]{2,1,0:T(8,128)(2,1)S(1)}, bf16[2,80,384]{2,1,0:T(8,128)(2,1)S(1)}, u32[]{:S(2)}, u32[]{:S(2)}) collective-permute-start(bf16[2,80,384]{2,1,0:T(8,128)(2,1)S(1)} %get-tuple-element.16), channel_id=1, source_target_pairs={{0,1},{1,0},{2,3},{3,2},{4,5},{5,4},{6,7},{7,6},{8,9},{9,8},{10,11... | collective-permute-start | bytes 368648 | tf_op jit(solution)/shard_map/ppermute | solution.py:321
  37.8 3.8 %collective-permute-start.3 = (f32[40,128]{1,0:T(8,128)S(1)}, f32[40,128]{1,0:T(8,128)S(1)}, u32[]{:S(2)}, u32[]{:S(2)}) collective-permute-start(f32[40,128]{1,0:T(8,128)S(1)} %shard_map.102.own_ref), channel_id=1, source_target_pairs={{0,248},{8,16},{16,8},{24,32},{32,24},{40,48},{48,40},{56,64},{64,... | collective-permute-start | bytes 61448 | tf_op jit(solution)/shard_map/ppermute | solution.py:366
  38.0 4.2 %collective-permute-start.2 = (f32[40,128]{1,0:T(8,128)S(1)}, f32[40,128]{1,0:T(8,128)S(1)}, u32[]{:S(2)}, u32[]{:S(2)}) collective-permute-start(f32[40,128]{1,0:T(8,128)S(1)} %shard_map.102.own_ref), channel_id=1, source_target_pairs={{0,8},{8,0},{16,24},{24,16},{32,40},{40,32},{48,56},{56,48},{64,72... | collective-permute-start | bytes 61448 | tf_op jit(solution)/shard_map/ppermute | solution.py:367

commit v7 on v5

--- a/solution.py
+++ b/solution.py
@@ -131,6 +131,7 @@
     gain_ref,
     first_ref,
     obs_ref,
+    bottom_ref,
     held,
     updated,
     gain,
@@ -159,6 +160,7 @@
     for m in range(2):
         pointwise(updated[m], gain_ref[:, :1], first_ref[...], second_ref[...], held, m)
     pack_rows(held, (0, ROW_PACK), out_ref)
+    bottom_ref[...] = x_ref[:, ROWS - 1]
     for copy in copies[1:]:
         copy.wait()
     slots = lax.broadcasted_iota(jnp.int32, (1, OBS), 1)
@@ -172,8 +174,8 @@
 def outer_kernel(
     band_ref,
     x_ref,
-    chip_ref,
-    next_ref,
+    low_ref,
+    high_ref,
     inner_ref,
     conv_ref,
     gain_ref,
@@ -183,13 +185,10 @@
     held,
 ):
     band = band_ref[...]
-    odd = band % 2 == 1
     windows = []
     for m in range(2):
-        chip = chip_ref[m].astype(F32)
-        beyond = next_ref[m].astype(F32)
-        low = jnp.where(band == 0, 0.0, jnp.where(odd, chip, beyond)).astype(BF16)
-        high = jnp.where(band == BANDS - 1, 0.0, jnp.where(odd, beyond, chip)).astype(BF16)
+        low = jnp.where(band == 0, 0.0, low_ref[m].astype(F32)).astype(BF16)
+        high = jnp.where(band == BANDS - 1, 0.0, high_ref[m].astype(F32)).astype(BF16)
         windows.append([[low, x_ref[m, 0], x_ref[m, 1]], [x_ref[m, 2], x_ref[m, 3], high]])
     for m in range(2):
         updated = convolve(windows[m], conv_ref[...])
@@ -310,12 +309,8 @@
     fields = jnp.pad(starting_fields.transpose(0, 2, 1, 3), ((0, 0), (0, 0), (0, 0), (0, WIDE - LON)))
     fields = lax.optimization_barrier(fields)
     band = lax.axis_index("space")
-    odd = band % 2
-    top, bottom = fields[:, 0], fields[:, ROWS - 1]
-    across = [(i, (i + 1 if i % 2 else i - 1) % BANDS) for i in range(BANDS)]
-    next_row = lax.ppermute(jnp.where(odd == 1, bottom, top), "space", across)
-    within = [(i, i ^ 1) for i in range(BANDS)]
-    chip_row = lax.ppermute(jnp.where(odd == 1, top, bottom), "space", within)
+    south = [((i + 1) % BANDS, i) for i in range(BANDS)]
+    high = lax.ppermute(fields[:, 0], "space", south)
     held = [pltpu.VMEM((2, 2, CHANNELS, WIDE), F32)]
     second = weight_out[0]
     small = [
@@ -325,7 +320,7 @@
         (obs_value[0], F32, (1, OBS)),
         (obs_precision[0], F32, (1, OBS)),
     ]
-    inner, conv, gain, first, observations = call(
+    inner, conv, gain, first, observations, bottom = call(
         inner_kernel,
         (
             jax.ShapeDtypeStruct((2 * ROW_PACK, PACK), BF16),
@@ -333,6 +328,7 @@
             jax.ShapeDtypeStruct((CHANNELS, 128), F32),
             jax.ShapeDtypeStruct((HID, CHANNELS), BF16),
             jax.ShapeDtypeStruct((8, OBS), F32),
+            jax.ShapeDtypeStruct((2, CHANNELS, WIDE), BF16),
         ),
         fields,
         conv_weight,
@@ -348,9 +344,10 @@
         cost_estimate=pl.CostEstimate(flops=400_000_000, bytes_accessed=2_000_000, transcendentals=500_000),
     )
     weights = (conv, gain, first, second)
+    low = lax.ppermute(bottom, "space", [(j, i) for i, j in south])
     packed = jax.ShapeDtypeStruct((PACK, PACK), BF16)
     sent = call(
-        outer_kernel, packed, band.reshape(1, 1), fields, chip_row, next_row, inner, *weights, scratch_shapes=held
+        outer_kernel, packed, band.reshape(1, 1), fields, low, high, inner, *weights, scratch_shapes=held
     )
 
     def exchange(block):

time: 69.8 us -> 70.3 us (level)
  waiting for transfers between devices: 2.66 us -> 5.88 us
  blocking collectives: 53.2 us -> 51 us
    ppermute x2, waiting for transfers between devices: 0.9 us -> 4.06 us  [the longest x1 4.06 us: body(): low = lax.ppermute(bottom, 'space', [(j, i) for i, j in south])]
    all_to_all x2, blocking collectives: 53.2 us -> 51 us  [exchange(): lax.all_to_all(block, 'member', split_axis=0, concat_axis=0, tiled=True)]
where the time goes in v7:
time: 70.3 us; the launch traced here: 70.1 us
  blocking collectives  51 us (73%)
  Pallas kernels  8.36 us (12%)
  waiting for transfers between devices  5.88 us (8%)
  starting transfers between devices  2.84 us (4%)
  local copies, waits for them, and re-layouts  1.23 us (2%)
  between operations  0.75 us (1%)
    all_to_all x2, blocking collectives, exchange(): lax.all_to_all(block, 'member', split_axis=0, concat_axis=0, tiled=True)  51 us
    pallas_call x5, Pallas kernels, call(): pl.pallas_call(kernel, out_shape=out_shape, compiler_params=pltpu.Compile...  8.36 us
    ppermute x1, waiting for transfers between devices, body(): low = lax.ppermute(bottom, 'space', [(j, i) for i, j in south])  4.06 us
    ppermute x1, starting transfers between devices, body(): near = lax.ppermute(own, 'member', [(i, i ^ 1) for i in range(around)])  1.97 us
    ppermute x1, waiting for transfers between devices, body(): lax.ppermute(own, 'member', [(i, (i + 1 if i % 2 else i - 1) % around) fo...  1.54 us
  transfers between devices with their start and end apart: 4, of which 3 were waited for; matrix products, arithmetic and copies ran while one was open for 0% of the time, Pallas kernels for 3%

profile of v7, /device:TPU:38, one launch (start us, length us, event | category | flops | bytes accessed | tf_op | source)
XLA Modules:
  0.0 70.1 jit_solution(466996212015697175)
XLA Ops:
  0.0 1.1 %copy.15 = bf16[2,80,4,360]{3,1,0,2:T(8,128)(2,1)S(1)} copy(bf16[2,80,4,360]{3,2,1,0:T(4,128)(2,1)} %param.10) | data formatting | bytes 921600 | tf_op args[0]
  1.1 0.1 pad.4
  1.2 0.0 copy-start
  1.2 0.0 copy-start.1
  1.2 0.0 copy-start.2
  1.2 0.3 collective-permute-start.1
  1.5 0.1 copy.13.x_ref
  2.2 0.0 copy-done
  2.2 0.0 copy-done.1
  2.2 0.0 copy-done.2
  2.2 2.0 %shard_map.100 = (bf16[256,512]{1,0:T(8,128)(2,1)S(1)}, bf16[240,240]{1,0:T(8,128)(2,1)S(1)}, f32[80,128]{1,0:T(8,128)S(1)}, bf16[320,80]{1,0:T(8,128)(2,1)S(1)}...) custom-call(bf16[2,4,80,384]{3,2,1,0:T(8,128)(2,1)S(1)} %copy.13.x_ref, bf16[1,9,80,80]{3,2,1,0:T(8,128)(2,1)S(1)} %copy-done.1, ...), custom_call_target="tpu_custom_call" | custom-call | flops 400000000 | bytes 2000000 | tf_op jit(solution)/shard_map/pallas_call | solution.py:289
  4.2 0.3 collective-permute-start
  4.5 0.0 collective-permute-done.1.high_ref
  4.5 4.1 %collective-permute-done.low_ref = bf16[2,80,384]{2,1,0:T(8,128)(2,1)S(1)} collective-permute-done((bf16[2,80,384]{2,1,0:T(8,128)(2,1)S(1)}, bf16[2,80,384]{2,1,0:T(8,128)(2,1)S(1)}, u32[]{:S(2)}, u32[]{:S(2)}) %collective-permute-start) | collective-permute-done | bytes 122912 | tf_op jit(solution)/shard_map/ppermute | solution.py:347
  8.6 1.8 %shard_map.101 = bf16[512,512]{1,0:T(8,128)(2,1)S(1)} custom-call(s32[1,1]{1,0:T(1,128)} %bitcast.band_ref, bf16[2,4,80,384]{3,2,1,0:T(8,128)(2,1)S(1)} %copy.13.x_ref, bf16[2,80,384]{2,1,0:T(8,128)(2,1)S(1)} %collective-permute-done.low_ref, bf16[2,80,384]{2,1,0:T(8,128)(2,1)S(1)} %collective-permute-done.1.high_ref, ...), custom_call_target="tpu_custom_call" | custom-call | tf_op jit(solution)/shard_map/pallas_call | solution.py:289
  10.4 29.0 %all_to_all.10 = bf16[32,16,512]{2,1,0:T(8,128)(2,1)S(1)} all-to-all(bf16[32,16,512]{2,1,0:T(8,128)(2,1)S(1)} %bitcast.22), channel_id=1, replica_groups=mesh['member'=32,'space'=8] {'member'}, dimensions={0} | all-to-all | bytes 1048576 | tf_op jit(solution)/shard_map/all_to_all | solution.py:355
  39.4 0.6 shard_map.102.own_ref
  40.0 0.3 collective-permute-start.3
  40.4 2.0 %collective-permute-start.2 = (f32[40,128]{1,0:T(8,128)S(1)}, f32[40,128]{1,0:T(8,128)S(1)}, u32[]{:S(2)}, u32[]{:S(2)}) collective-permute-start(f32[40,128]{1,0:T(8,128)S(1)} %shard_map.102.own_ref), channel_id=1, source_target_pairs={{0,8},{8,0},{16,24},{24,16},{32,40},{40,32},{48,56},{56,48},{64,72... | collective-permute-start | bytes 61448 | tf_op jit(solution)/shard_map/ppermute | solution.py:362
  42.3 1.5 %collective-permute-done.3.far_ref = f32[40,128]{1,0:T(8,128)S(1)} collective-permute-done((f32[40,128]{1,0:T(8,128)S(1)}, f32[40,128]{1,0:T(8,128)S(1)}, u32[]{:S(2)}, u32[]{:S(2)}) %collective-permute-start.3) | collective-permute-done | bytes 20512 | tf_op jit(solution)/shard_map/ppermute | solution.py:361
  43.9 0.3 collective-permute-done.2.near_ref
  44.2 2.5 %shard_map.103 = bf16[512,512]{1,0:T(8,128)(2,1)S(1)} custom-call(f32[40,128]{1,0:T(8,128)S(1)} %shard_map.102.own_ref, f32[40,128]{1,0:T(8,128)S(1)} %collective-permute-done.2.near_ref, f32[40,128]{1,0:T(8,128)S(1)} %collective-permute-done.3.far_ref, bf16[512,512]{1,0:T(8,128)(2,1)S(1)} %bitcast.19), custom_call_target="tpu_custom_call" | custom-call | tf_op jit(solution)/shard_map/pallas_call | solution.py:289
  46.7 22.0 %all_to_all.11 = bf16[32,16,512]{2,1,0:T(8,128)(2,1)S(1)} all-to-all(bf16[32,16,512]{2,1,0:T(8,128)(2,1)S(1)} %bitcast.20), channel_id=1, replica_groups=mesh['member'=32,'space'=8] {'member'}, dimensions={0} | all-to-all | bytes 1048576 | tf_op jit(solution)/shard_map/all_to_all | solution.py:355
  68.7 1.4 %shard_map.104 = bf16[2,80,4,360]{3,2,1,0:T(4,128)(2,1)} custom-call(bf16[512,512]{1,0:T(8,128)(2,1)S(1)} %bitcast.21), custom_call_target="tpu_custom_call" | custom-call | tf_op jit(solution)/shard_map/pallas_call | solution.py:289
  (1 shorter events, 0.0 us)
Async XLA Ops:
  1.2 1.0 %copy-start = (bf16[1,80,320]{2,1,0:T(8,128)(2,1)S(1)}, bf16[1,80,320]{2,1,0:T(8,128)(2,1)}, u32[]{:S(2)}) copy-start(bf16[1,80,320]{2,1,0:T(8,128)(2,1)} %param.14) | copy-start | bytes 153604
  1.2 1.0 %copy-start.1 = (bf16[1,9,80,80]{3,2,1,0:T(8,128)(2,1)S(1)}, bf16[1,9,80,80]{3,2,1,0:T(8,128)(2,1)}, u32[]{:S(2)}) copy-start(bf16[1,9,80,80]{3,2,1,0:T(8,128)(2,1)} %conv.1) | copy-start | bytes 345604
  1.2 1.0 %copy-start.2 = (bf16[1,320,80]{1,2,0:T(8,128)(2,1)S(1)}, bf16[1,320,80]{1,2,0:T(8,128)(2,1)}, u32[]{:S(2)}) copy-start(bf16[1,320,80]{1,2,0:T(8,128)(2,1)} %param.13) | copy-start | bytes 153604
  1.2 3.3 %collective-permute-start.1 = (bf16[2,80,384]{2,1,0:T(8,128)(2,1)S(1)}, bf16[2,80,384]{2,1,0:T(8,128)(2,1)S(1)}, u32[]{:S(2)}, u32[]{:S(2)}) collective-permute-start(bf16[2,80,384]{2,1,0:T(8,128)(2,1)S(1)} %slice_bitcast_fusion), channel_id=1, source_target_pairs={{1,0},{2,1},{3,2},{4,3},{5,4},{6,5},{7,6},{0,7},{9,8},{10,9},{11,1... | collective-permute-start | bytes 368648 | tf_op jit(solution)/shard_map/ppermute | solution.py:313
  4.2 4.3 %collective-permute-start = (bf16[2,80,384]{2,1,0:T(8,128)(2,1)S(1)}, bf16[2,80,384]{2,1,0:T(8,128)(2,1)S(1)}, u32[]{:S(2)}, u32[]{:S(2)}) collective-permute-start(bf16[2,80,384]{2,1,0:T(8,128)(2,1)S(1)} %get-tuple-element.11), channel_id=1, source_target_pairs={{0,1},{1,2},{2,3},{3,4},{4,5},{5,6},{6,7},{7,0},{8,9},{9,10},{10,1... | collective-permute-start | bytes 368648 | tf_op jit(solution)/shard_map/ppermute | solution.py:347
  40.0 3.8 %collective-permute-start.3 = (f32[40,128]{1,0:T(8,128)S(1)}, f32[40,128]{1,0:T(8,128)S(1)}, u32[]{:S(2)}, u32[]{:S(2)}) collective-permute-start(f32[40,128]{1,0:T(8,128)S(1)} %shard_map.102.own_ref), channel_id=1, source_target_pairs={{0,248},{8,16},{16,8},{24,32},{32,24},{40,48},{48,40},{56,64},{64,... | collective-permute-start | bytes 61448 | tf_op jit(solution)/shard_map/ppermute | solution.py:361
  40.4 3.8 %collective-permute-start.2 = (f32[40,128]{1,0:T(8,128)S(1)}, f32[40,128]{1,0:T(8,128)S(1)}, u32[]{:S(2)}, u32[]{:S(2)}) collective-permute-start(f32[40,128]{1,0:T(8,128)S(1)} %shard_map.102.own_ref), channel_id=1, source_target_pairs={{0,8},{8,0},{16,24},{24,16},{32,40},{40,32},{48,56},{56,48},{64,72... | collective-permute-start | bytes 61448 | tf_op jit(solution)/shard_map/ppermute | solution.py:362

commit v8 on v5

--- a/solution.py
+++ b/solution.py
@@ -88,14 +88,12 @@
     return jnp.concatenate(parts, axis=1)
 
 
-def pointwise(updated, gain, first, second, held, m):
+def pointwise(updated, gain, first, second):
     power = jnp.sum(updated * updated, axis=0, keepdims=True) * (1.0 / CHANNELS)
     normed = (updated * lax.rsqrt(power + EPSILON) * gain).astype(BF16)
     hidden = mm(first, normed)
     hidden = (hidden * (0.5 + 0.5 * jnp.tanh(0.5 * hidden))).astype(BF16)
-    result = updated + mm(second, hidden)
-    held[0, m] = result[:, :WIDE]
-    held[1, m] = result[:, WIDE:]
+    return updated + mm(second, hidden)
 
 
 def pack_rows(held, starts, out_ref):
@@ -157,7 +155,9 @@
     tall = jnp.sum(jnp.where(row == column, gain[...], 0.0), axis=1, keepdims=True)
     gain_ref[...] = jnp.broadcast_to(tall, (CHANNELS, 128))
     for m in range(2):
-        pointwise(updated[m], gain_ref[:, :1], first_ref[...], second_ref[...], held, m)
+        result = pointwise(updated[m], gain_ref[:, :1], first_ref[...], second_ref[...])
+        held[0, m] = result[:, :WIDE]
+        held[1, m] = result[:, WIDE:]
     pack_rows(held, (0, ROW_PACK), out_ref)
     for copy in copies[1:]:
         copy.wait()
@@ -169,33 +169,47 @@
     obs_ref[4:, :] = jnp.zeros((4, OBS), F32)
 
 
-def outer_kernel(
-    band_ref,
-    x_ref,
-    chip_ref,
-    next_ref,
-    inner_ref,
-    conv_ref,
-    gain_ref,
-    first_ref,
-    second_ref,
-    out_ref,
-    held,
+def edge_rows(windows, conv_ref, gain_ref, first_ref, second_ref, held, out_ref, start):
+    updated = convolve(windows, conv_ref[...])
+    gain = gain_ref[:, :1]
+    result = pointwise(updated, gain, first_ref[...], second_ref[...])
+    for m in range(2):
+        held[0, m] = result[:, m * WIDE : (m + 1) * WIDE]
+    pack_rows(held, (start,), out_ref)
+
+
+def either(choice, left, right):
+    return jnp.where(choice, left.astype(F32), right.astype(F32)).astype(BF16)
+
+
+def chip_kernel(band_ref, x_ref, chip_ref, conv_ref, gain_ref, first_ref, second_ref, out_ref, held):
+    odd = band_ref[...] % 2 == 1
+    windows = []
+    for m in range(2):
+        above = either(odd, chip_ref[m], x_ref[m, ROWS - 2])
+        here = either(odd, x_ref[m, 0], x_ref[m, ROWS - 1])
+        below = either(odd, x_ref[m, 1], chip_ref[m])
+        windows.append([above, here, below])
+    edge_rows(windows, conv_ref, gain_ref, first_ref, second_ref, held, out_ref, 0)
+
+
+def next_kernel(
+    band_ref, x_ref, next_ref, inner_ref, chip_ref, conv_ref, gain_ref, first_ref, second_ref, out_ref, held, edge
 ):
     band = band_ref[...]
     odd = band % 2 == 1
+    outside = (band == 0) | (band == BANDS - 1)
     windows = []
     for m in range(2):
-        chip = chip_ref[m].astype(F32)
-        beyond = next_ref[m].astype(F32)
-        low = jnp.where(band == 0, 0.0, jnp.where(odd, chip, beyond)).astype(BF16)
-        high = jnp.where(band == BANDS - 1, 0.0, jnp.where(odd, beyond, chip)).astype(BF16)
-        windows.append([[low, x_ref[m, 0], x_ref[m, 1]], [x_ref[m, 2], x_ref[m, 3], high]])
-    for m in range(2):
-        updated = convolve(windows[m], conv_ref[...])
-        pointwise(updated, gain_ref[:, :1], first_ref[...], second_ref[...], held, m)
-    pack_rows(held, (0, 3 * ROW_PACK), out_ref)
+        beyond = jnp.where(outside, 0.0, next_ref[m].astype(F32)).astype(BF16)
+        above = either(odd, x_ref[m, ROWS - 2], beyond)
+        here = either(odd, x_ref[m, ROWS - 1], x_ref[m, 0])
+        below = either(odd, beyond, x_ref[m, 1])
+        windows.append([above, here, below])
+    edge_rows(windows, conv_ref, gain_ref, first_ref, second_ref, held, edge, 0)
+    out_ref[:ROW_PACK, :] = either(odd, chip_ref[...], edge[...])
     out_ref[ROW_PACK : 3 * ROW_PACK, :] = inner_ref[...]
+    out_ref[3 * ROW_PACK :, :] = either(odd, edge[...], chip_ref[...])
 
 
 def observe_kernel(tile_ref, obs_ref, out_ref):
@@ -349,8 +363,27 @@
     )
     weights = (conv, gain, first, second)
     packed = jax.ShapeDtypeStruct((PACK, PACK), BF16)
+    band = band.reshape(1, 1)
+    beside = call(
+        chip_kernel,
+        jax.ShapeDtypeStruct((ROW_PACK, PACK), BF16),
+        band,
+        fields,
+        chip_row,
+        *weights,
+        scratch_shapes=held,
+        cost_estimate=pl.CostEstimate(flops=200_000_000, bytes_accessed=1_000_000, transcendentals=250_000),
+    )
     sent = call(
-        outer_kernel, packed, band.reshape(1, 1), fields, chip_row, next_row, inner, *weights, scratch_shapes=held
+        next_kernel,
+        packed,
+        band,
+        fields,
+        next_row,
+        inner,
+        beside,
+        *weights,
+        scratch_shapes=held + [pltpu.VMEM((ROW_PACK, PACK), BF16)],
     )
 
     def exchange(block):

time: 69.8 us -> 69.8 us (level)
  waiting for transfers between devices: 2.66 us -> 1.76 us
    ppermute x1, waiting for transfers between devices: 0.9 us -> 0.01 us  [body(): next_row = lax.ppermute(jnp.where(odd == 1, bottom, top), 'space', across)]
    pallas_call x5 -> x6, Pallas kernels: 8.45 us -> 8.87 us  [call(): pl.pallas_call(kernel, out_shape=out_shape, compiler_params=pltpu.Compile...]
  transfers between devices with their start and end apart: 4 -> 4, of which waited for: 3 -> 2; matrix products, arithmetic and copies ran while one was open for 0% -> 0% of each run, Pallas kernels for 3% -> 5%
where the time goes in v8:
time: 69.8 us; the launch traced here: 69.6 us
  blocking collectives  53.3 us (76%)
  Pallas kernels  8.87 us (13%)
  starting transfers between devices  3.62 us (5%)
  waiting for transfers between devices  1.76 us (3%)
  local copies, waits for them, and re-layouts  1.22 us (2%)
  between operations  0.78 us (1%)
    all_to_all x2, blocking collectives, exchange(): lax.all_to_all(block, 'member', split_axis=0, concat_axis=0, tiled=True)  53.3 us
    pallas_call x6, Pallas kernels, call(): pl.pallas_call(kernel, out_shape=out_shape, compiler_params=pltpu.Compile...  8.87 us
    ppermute x1, starting transfers between devices, body(): near = lax.ppermute(own, 'member', [(i, i ^ 1) for i in range(around)])  2.54 us
  transfers between devices with their start and end apart: 4, of which 2 were waited for; matrix products, arithmetic and copies ran while one was open for 0% of the time, Pallas kernels for 5%

profile of v8, /device:TPU:38, one launch (start us, length us, event | category | flops | bytes accessed | tf_op | source)
XLA Modules:
  0.0 69.6 jit_solution(5781093213652531593)
XLA Ops:
  0.0 1.1 %copy.16 = bf16[2,80,4,360]{3,1,0,2:T(8,128)(2,1)S(1)} copy(bf16[2,80,4,360]{3,2,1,0:T(4,128)(2,1)} %param.10) | data formatting | bytes 921600 | tf_op args[0]
  1.1 0.1 pad.4
  1.2 0.1 collective-permute-start.1
  1.3 0.0 copy-start
  1.3 0.0 copy-start.1
  1.3 0.0 copy-start.2
  1.3 0.9 %collective-permute-start = (bf16[2,80,384]{2,1,0:T(8,128)(2,1)S(1)}, bf16[2,80,384]{2,1,0:T(8,128)(2,1)S(1)}, u32[]{:S(2)}, u32[]{:S(2)}) collective-permute-start(bf16[2,80,384]{2,1,0:T(8,128)(2,1)S(1)} %get-tuple-element.16), channel_id=1, source_target_pairs={{0,7},{1,2},{2,1},{3,4},{4,3},{5,6},{6,5},{7,0},{8,15},{9,10},{10,... | collective-permute-start | bytes 368648 | tf_op jit(solution)/shard_map/ppermute | solution.py:330
  2.2 0.1 copy.14.x_ref
  2.9 0.0 copy-done
  2.9 0.0 copy-done.1
  3.0 2.1 %shard_map.100 = (bf16[256,512]{1,0:T(8,128)(2,1)S(1)}, bf16[240,240]{1,0:T(8,128)(2,1)S(1)}, f32[80,128]{1,0:T(8,128)S(1)}, bf16[320,80]{1,0:T(8,128)(2,1)S(1)}, f32[8,256]{1,0:T(8,128)S(1)}) custom-call(bf16[2,4,80,384]{3,2,1,0:T(8,128)(2,1)S(1)} %copy.14.x_ref, bf16[1,9,80,80]{3,2,1,0:T(8,128)(2,1)S(1)} %copy-done.1, bf16[80,320]{1,0:T(8,128)(2,1)S(1)} %bitcast.28, ...), custom_call_target="tpu_custom_call" | custom-call | flops 400000000 | bytes 2000000 | tf_op jit(solution)/shard_map/pallas_call | solution.py:304
  5.0 0.0 collective-permute-done.1.chip_ref
  5.1 1.1 %shard_map.101.chip_ref = bf16[128,512]{1,0:T(8,128)(2,1)S(1)} custom-call(s32[1,1]{1,0:T(1,128)} %bitcast.band_ref, bf16[2,4,80,384]{3,2,1,0:T(8,128)(2,1)S(1)} %copy.14.x_ref, bf16[2,80,384]{2,1,0:T(8,128)(2,1)S(1)} %collective-permute-done.1.chip_ref, bf16[240,240]{1,0:T(8,128)(2,1)S(1)} %get-tuple-element.11.conv_ref, ...), custom_call_target="tpu_custom_call" | custom-call | flops 200000000 | bytes 1000000 | tf_op jit(solution)/shard_map/pallas_call | solution.py:304
  6.2 0.0 collective-permute-done.next_ref
  6.2 1.1 %shard_map.102 = bf16[512,512]{1,0:T(8,128)(2,1)S(1)} custom-call(s32[1,1]{1,0:T(1,128)} %bitcast.band_ref, bf16[2,4,80,384]{3,2,1,0:T(8,128)(2,1)S(1)} %copy.14.x_ref, bf16[2,80,384]{2,1,0:T(8,128)(2,1)S(1)} %collective-permute-done.next_ref, bf16[256,512]{1,0:T(8,128)(2,1)S(1)} %get-tuple-element.10.inner_ref, bf16[128,512]{1,0:T(8,128)(2,1)S(1)} %shard_map.101.chip_ref, ...), custom_call_target="tpu_custom_call" | custom-call | tf_op jit(solution)/shard_map/pallas_call | solution.py:304
  7.3 29.9 %all_to_all.10 = bf16[32,16,512]{2,1,0:T(8,128)(2,1)S(1)} all-to-all(bf16[32,16,512]{2,1,0:T(8,128)(2,1)S(1)} %bitcast.24), channel_id=1, replica_groups=mesh['member'=32,'space'=8] {'member'}, dimensions={0} | all-to-all | bytes 1048576 | tf_op jit(solution)/shard_map/all_to_all | solution.py:391
  37.2 0.6 shard_map.103.own_ref
  37.8 0.1 collective-permute-start.3
  37.9 2.5 %collective-permute-start.2 = (f32[40,128]{1,0:T(8,128)S(1)}, f32[40,128]{1,0:T(8,128)S(1)}, u32[]{:S(2)}, u32[]{:S(2)}) collective-permute-start(f32[40,128]{1,0:T(8,128)S(1)} %shard_map.103.own_ref), channel_id=1, source_target_pairs={{0,8},{8,0},{16,24},{24,16},{32,40},{40,32},{48,56},{56,48},{64,72... | collective-permute-start | bytes 61448 | tf_op jit(solution)/shard_map/ppermute | solution.py:398
  40.5 1.2 %collective-permute-done.3.far_ref = f32[40,128]{1,0:T(8,128)S(1)} collective-permute-done((f32[40,128]{1,0:T(8,128)S(1)}, f32[40,128]{1,0:T(8,128)S(1)}, u32[]{:S(2)}, u32[]{:S(2)}) %collective-permute-start.3) | collective-permute-done | bytes 20512 | tf_op jit(solution)/shard_map/ppermute | solution.py:397
  41.7 0.5 collective-permute-done.2.near_ref
  42.2 2.5 %shard_map.104 = bf16[512,512]{1,0:T(8,128)(2,1)S(1)} custom-call(f32[40,128]{1,0:T(8,128)S(1)} %shard_map.103.own_ref, f32[40,128]{1,0:T(8,128)S(1)} %collective-permute-done.2.near_ref, f32[40,128]{1,0:T(8,128)S(1)} %collective-permute-done.3.far_ref, bf16[512,512]{1,0:T(8,128)(2,1)S(1)} %bitcast.21), custom_call_target="tpu_custom_call" | custom-call | tf_op jit(solution)/shard_map/pallas_call | solution.py:304
  44.8 23.4 %all_to_all.11 = bf16[32,16,512]{2,1,0:T(8,128)(2,1)S(1)} all-to-all(bf16[32,16,512]{2,1,0:T(8,128)(2,1)S(1)} %bitcast.22), channel_id=1, replica_groups=mesh['member'=32,'space'=8] {'member'}, dimensions={0} | all-to-all | bytes 1048576 | tf_op jit(solution)/shard_map/all_to_all | solution.py:391
  68.2 1.4 %shard_map.105 = bf16[2,80,4,360]{3,2,1,0:T(4,128)(2,1)} custom-call(bf16[512,512]{1,0:T(8,128)(2,1)S(1)} %bitcast.23), custom_call_target="tpu_custom_call" | custom-call | tf_op jit(solution)/shard_map/pallas_call | solution.py:304
  (2 shorter events, 0.0 us)
Async XLA Ops:
  1.2 3.9 %collective-permute-start.1 = (bf16[2,80,384]{2,1,0:T(8,128)(2,1)S(1)}, bf16[2,80,384]{2,1,0:T(8,128)(2,1)S(1)}, u32[]{:S(2)}, u32[]{:S(2)}) collective-permute-start(bf16[2,80,384]{2,1,0:T(8,128)(2,1)S(1)} %get-tuple-element.15), channel_id=1, source_target_pairs={{0,1},{1,0},{2,3},{3,2},{4,5},{5,4},{6,7},{7,6},{8,9},{9,8},{10,11... | collective-permute-start | bytes 368648 | tf_op jit(solution)/shard_map/ppermute | solution.py:332
  1.3 1.6 %copy-start = (bf16[1,80,320]{2,1,0:T(8,128)(2,1)S(1)}, bf16[1,80,320]{2,1,0:T(8,128)(2,1)}, u32[]{:S(2)}) copy-start(bf16[1,80,320]{2,1,0:T(8,128)(2,1)} %param.14) | copy-start | bytes 153604
  1.3 1.6 %copy-start.1 = (bf16[1,9,80,80]{3,2,1,0:T(8,128)(2,1)S(1)}, bf16[1,9,80,80]{3,2,1,0:T(8,128)(2,1)}, u32[]{:S(2)}) copy-start(bf16[1,9,80,80]{3,2,1,0:T(8,128)(2,1)} %conv.1) | copy-start | bytes 345604
  1.3 1.6 %copy-start.2 = (bf16[1,320,80]{1,2,0:T(8,128)(2,1)S(1)}, bf16[1,320,80]{1,2,0:T(8,128)(2,1)}, u32[]{:S(2)}) copy-start(bf16[1,320,80]{1,2,0:T(8,128)(2,1)} %param.13) | copy-start | bytes 153604
  1.3 4.8 %collective-permute-start = (bf16[2,80,384]{2,1,0:T(8,128)(2,1)S(1)}, bf16[2,80,384]{2,1,0:T(8,128)(2,1)S(1)}, u32[]{:S(2)}, u32[]{:S(2)}) collective-permute-start(bf16[2,80,384]{2,1,0:T(8,128)(2,1)S(1)} %get-tuple-element.16), channel_id=1, source_target_pairs={{0,7},{1,2},{2,1},{3,4},{4,3},{5,6},{6,5},{7,0},{8,15},{9,10},{10,... | collective-permute-start | bytes 368648 | tf_op jit(solution)/shard_map/ppermute | solution.py:330
  37.8 3.8 %collective-permute-start.3 = (f32[40,128]{1,0:T(8,128)S(1)}, f32[40,128]{1,0:T(8,128)S(1)}, u32[]{:S(2)}, u32[]{:S(2)}) collective-permute-start(f32[40,128]{1,0:T(8,128)S(1)} %shard_map.103.own_ref), channel_id=1, source_target_pairs={{0,248},{8,16},{16,8},{24,32},{32,24},{40,48},{48,40},{56,64},{64,... | collective-permute-start | bytes 61448 | tf_op jit(solution)/shard_map/ppermute | solution.py:397
  37.9 4.3 %collective-permute-start.2 = (f32[40,128]{1,0:T(8,128)S(1)}, f32[40,128]{1,0:T(8,128)S(1)}, u32[]{:S(2)}, u32[]{:S(2)}) collective-permute-start(f32[40,128]{1,0:T(8,128)S(1)} %shard_map.103.own_ref), channel_id=1, source_target_pairs={{0,8},{8,0},{16,24},{24,16},{32,40},{40,32},{48,56},{56,48},{64,72... | collective-permute-start | bytes 61448 | tf_op jit(solution)/shard_map/ppermute | solution.py:398
